TPU v7x, 256 devices: a whole 4x4x8 slice. The times are simulated.
256 devices in a mesh: seq: 128 (over y, x, z), dp: 2 (over core).
Axes of the slice: x: 4, y: 4, z: 8, core: 2. Of those that a mesh axis runs over, the one named last changes fastest.
Arguments:
- byte_states: bfloat16 [2, 16384, 4096], P('dp', 'seq'), may hold values from -8 to 8
- patch_starts: int32 [2, 4096], P('dp', 'seq'), may hold values from 0 to 16383, as said below
- patch_lengths: int32 [2, 4096], P('dp', 'seq'), may hold values from 1 to 7, as said below
- query_gain: float32 [4096], replicated, may hold values from 0.1 to 1.9
- key_gain: float32 [4096], replicated, may hold values from 0.1 to 1.9
- out_cotangent: bfloat16 [2, 4096, 4096], P('dp', 'seq'), may hold values from -6 to 6
Outputs:
- patch_out: bfloat16 [2, 4096, 4096], P('dp', 'seq')
- grad_bytes: float32 [2, 16384, 4096], P('dp', 'seq')
- grad_qgain: float32 [4096], replicated
- grad_kgain: float32 [4096], replicated
Inputs may be any that keep to these rules, and one draw needn't show every extreme that they name: `patch_starts`: each device's bytes hold the starts of exactly 32 patches; starts rise, the first is 0, and each patch ends where the next starts (the last at the document's end), so a patch may run into the next device's bytes. patch_lengths[p] = patch_starts[p + 1] - patch_starts[p], and the document's end for the last patch.
All inputs are finite; a program needn't handle non-finite values.
Results may differ from a plain program's by a relative error of at most 0.0075.
The roundings to bfloat16 on the way count: a program that leaves them out, or rounds other values in their place, can miss the bound.
Values may be sent and summed in bfloat16 or wider, within the bound.
A program may use at most 128 MiB of HBM per device.

v0:
```python
import jax
import jax.numpy as jnp
from jax import lax
from jax.sharding import PartitionSpec as P

HEAD_DIM = 128
MAXLEN = 8


EPSILON = 1e-06


def passed_along(value, axis, steps):
    count = lax.axis_size(axis)
    first, last = (max(0, -steps), min(count, count - steps))
    return lax.ppermute(value, axis, [(source, source + steps) for source in range(first, last)])


def from_behind(value, axis, steps):
    count = lax.axis_size(axis)
    pairs = [(source, (source + steps) % count) for source in range(count)]
    return lax.ppermute(value, axis, pairs)


def as_sent(array):

    def short(part):
        return part.astype(jnp.bfloat16) if part.dtype == jnp.float32 else part

    return jax.tree.map(short, array)


def to_heads_layout(array, heads, width):
    rows = array.shape[0]
    return (
        array.reshape(4, rows // 4, heads, width)
        .transpose(0, 2, 1, 3)
        .reshape(4 * heads, rows // 4, width)
    )


def from_heads_layout(array, heads, width):
    quarter_rows = array.shape[1]
    return (
        array.reshape(4, heads, quarter_rows, width)
        .transpose(0, 2, 1, 3)
        .reshape(4 * quarter_rows, heads * width)
    )


def attend_block(carry, items, keyed, values, key_ids, scale):
    dkey_total, dvalue_total = carry
    query, incoming, query_ids = items
    scores = jnp.dot(query, keyed.T, preferred_element_type=jnp.float32) * scale
    scores = jnp.where(key_ids[None, :] <= query_ids[:, None], scores, -1e30)
    top = jnp.max(scores, -1, keepdims=True)
    expo = jnp.exp(scores - top)
    probs = expo / jnp.sum(expo, -1, keepdims=True)
    weights = probs.astype(jnp.bfloat16)
    mixed = jnp.dot(weights, values, preferred_element_type=jnp.float32)
    spread = jnp.sqrt(jnp.mean(mixed * mixed, -1, keepdims=True) + EPSILON)
    result = (mixed / spread).astype(jnp.bfloat16)
    grad_in = incoming.astype(jnp.float32)
    dmixed = grad_in / spread - mixed * (
        jnp.sum(grad_in * mixed, -1, keepdims=True) / (HEAD_DIM * spread**3)
    )
    dmixed_b = dmixed.astype(jnp.bfloat16)
    dprobs = jnp.dot(dmixed_b, values.T, preferred_element_type=jnp.float32)
    dscores = probs * (dprobs - jnp.sum(probs * dprobs, -1, keepdims=True))
    dscaled = (dscores * scale).astype(jnp.bfloat16)
    dquery = jnp.dot(dscaled, keyed, preferred_element_type=jnp.float32)
    dkey_total = dkey_total + lax.dot_general(
        dscaled, query, (((0,), (0,)), ((), ())), preferred_element_type=jnp.float32
    )
    dvalue_total = dvalue_total + lax.dot_general(
        weights, dmixed_b, (((0,), (0,)), ((), ())), preferred_element_type=jnp.float32
    )
    return ((dkey_total, dvalue_total), (result, dquery))


def on_device(byte_states, patch_starts, patch_lengths, query_gain, key_gain, out_cotangent):
    states = byte_states[0]
    starts = patch_starts[0]
    lengths = patch_lengths[0]
    cotangent = out_cotangent[0]
    byte_rows, width_all = states.shape
    patch_rows = starts.shape[0]
    seq_count = lax.axis_size("seq")
    heads = seq_count // 4
    width = width_all // heads
    device = lax.axis_index("seq")
    head = device % heads
    quarter = device // heads
    spill = passed_along(states[:MAXLEN], "seq", -1)
    extended = jnp.concatenate([states, spill], 0)
    local_start = starts - device * byte_rows
    offsets = jnp.arange(byte_rows + MAXLEN, dtype=jnp.int32)
    inside = (offsets[None, :] >= local_start[:, None]) & (
        offsets[None, :] < (local_start + lengths)[:, None]
    )
    member = inside.astype(jnp.bfloat16)
    inverse_len = 1.0 / lengths.astype(jnp.float32)
    pooled = (
        jnp.dot(member, extended, preferred_element_type=jnp.float32) * inverse_len[:, None]
    ).astype(jnp.bfloat16)
    pooled_h, cot_h = (
        lax.all_to_all(
            to_heads_layout(pooled, heads, width), "seq", split_axis=0, concat_axis=1, tiled=True
        ),
        lax.all_to_all(
            to_heads_layout(cotangent, heads, width), "seq", split_axis=0, concat_axis=1, tiled=True
        ),
    )
    mine = pooled_h[0]
    grad_out = cot_h[0]
    quarter_rows = mine.shape[0]
    piece = patch_rows // 4
    row_order = jnp.arange(quarter_rows, dtype=jnp.int32)
    base_ids = row_order // piece * patch_rows + row_order % piece
    query_ids = base_ids + quarter * piece
    blocks = [mine]
    for distance in range(1, 4):
        blocks.append(from_behind(mine, "seq", distance * heads))
    values = jnp.concatenate(blocks, 0)
    key_ids = jnp.concatenate(
        [base_ids + (quarter - distance) % 4 * piece for distance in range(4)], 0
    )
    qgain_h = lax.dynamic_slice_in_dim(query_gain, head * width, width)
    kgain_h = lax.dynamic_slice_in_dim(key_gain, head * width, width)
    mine_f = mine.astype(jnp.float32)
    query = (mine_f * qgain_h).astype(jnp.bfloat16)
    keyed = (values.astype(jnp.float32) * kgain_h).astype(jnp.bfloat16)
    block = min(512, quarter_rows)
    count = quarter_rows // block
    scale = HEAD_DIM ** (-0.5)
    zero_keys = jnp.zeros((4 * quarter_rows, width), jnp.float32)

    def step_fn(carry, items):
        return attend_block(carry, items, keyed, values, key_ids, scale)

    (dkey_part, dvalue_part), (results, dquery) = lax.scan(
        step_fn,
        (zero_keys, zero_keys),
        (
            query.reshape(count, block, width),
            grad_out.reshape(count, block, width),
            query_ids.reshape(count, block),
        ),
    )
    results = results.reshape(quarter_rows, width)
    dquery = dquery.reshape(quarter_rows, width)
    key_side = dkey_part * kgain_h + dvalue_part
    parts = [
        key_side[distance * quarter_rows : (distance + 1) * quarter_rows] for distance in range(4)
    ]
    gathered = parts[0]
    for distance in range(1, 4):
        gathered = gathered + from_behind(
            parts[distance].astype(jnp.bfloat16), "seq", -distance * heads
        ).astype(jnp.float32)
    dpooled_h = dquery * qgain_h + gathered
    qgain_term = jnp.sum(dquery * mine_f, 0)
    kgain_term = jnp.sum(dkey_part * values.astype(jnp.float32), 0)
    output_rows = lax.all_to_all(results[None], "seq", split_axis=1, concat_axis=0, tiled=True)
    grad_rows = lax.all_to_all(
        as_sent(dpooled_h[None]), "seq", split_axis=1, concat_axis=0, tiled=True
    )
    patch_out = from_heads_layout(output_rows, heads, width)
    dpooled = from_heads_layout(grad_rows, heads, width)
    scaled = dpooled * inverse_len[:, None]
    extended_grad = jnp.dot(member.astype(jnp.float32).T, scaled, precision=lax.Precision.HIGHEST)
    spill_grad = passed_along(as_sent(extended_grad[byte_rows:]), "seq", 1)
    grad_local = extended_grad[:byte_rows] + jnp.pad(spill_grad, ((0, byte_rows - MAXLEN), (0, 0)))
    selector = (jnp.arange(heads, dtype=jnp.int32) == head).astype(jnp.float32)
    qgain_vec = (selector[:, None] * qgain_term[None, :]).reshape(width_all)
    kgain_vec = (selector[:, None] * kgain_term[None, :]).reshape(width_all)
    grad_qgain, grad_kgain = lax.psum((qgain_vec, kgain_vec), ("seq", "dp"))
    return (patch_out[None], grad_local[None], grad_qgain, grad_kgain)


def solution(mesh):
    placed = (P("dp", "seq", None), P("dp", "seq"), P("dp", "seq"), P(), P(), P("dp", "seq", None))
    return jax.shard_map(
        on_device,
        mesh=mesh,
        in_specs=placed,
        out_specs=(P("dp", "seq", None), P("dp", "seq", None), P(), P()),
        check_vma=False,
    )
```

profile of v0, /device:TPU:1, one launch (start us, length us, event | category | flops | bytes accessed | tf_op | source)
XLA Modules:
  0.0 271.0 jit_solution(700598147126363333)
XLA Ops:
  0.6 0.8 slice_bitcast_fusion
  1.5 1.3 collective-permute-start
  2.8 0.7 bitcast_add_fusion
  4.1 3.4 %collective-permute-done = bf16[8,4096]{1,0:T(8,128)(2,1)S(1)} collective-permute-done((bf16[8,4096]{1,0:T(8,128)(2,1)S(1)}, bf16[8,4096]{1,0:T(8,128)(2,1)S(1)}, u32[]{:S(2)}, u32[]{:S(2)}) %collective-permute-start) | collective-permute-done | bytes 65568 | tf_op jit(solution)/shard_map/ppermute | solution.py:16
  7.5 2.3 fusion.18
  9.8 17.9 %all-to-all-start = ((bf16[128,8,128]{2,1,0:T(8,128)(2,1)}), bf16[128,8,128]{2,1,0:T(8,128)(2,1)S(1)}, u32[]{:S(2)}, u32[]{:S(2)}) async-start(bf16[128,8,128]{2,1,0:T(8,128)(2,1)} %bitcast.6), calls=%async_computation | async-start | bytes 524288 | tf_op jit(solution)/shard_map/all_to_all | solution.py:107
  27.9 12.6 %all-to-all-done = bf16[128,8,128]{2,1,0:T(8,128)(2,1)S(1)} async-done(((bf16[128,8,128]{2,1,0:T(8,128)(2,1)}), bf16[128,8,128]{2,1,0:T(8,128)(2,1)S(1)}, u32[]{:S(2)}, u32[]{:S(2)}) %all-to-all-start) | async-done | bytes 262176 | tf_op jit(solution)/shard_map/all_to_all | solution.py:107
  40.5 7.3 %all-to-all-start.1 = ((bf16[128,8,128]{2,1,0:T(8,128)(2,1)}), bf16[128,8,128]{2,1,0:T(8,128)(2,1)}, u32[]{:S(2)}, u32[]{:S(2)}) async-start(bf16[128,8,128]{2,1,0:T(8,128)(2,1)} %bitcast.11), calls=%async_computation.1 | async-start | bytes 524288 | tf_op jit(solution)/shard_map/all_to_all | solution.py:110
  47.8 2.3 collective-permute-start.3
  50.3 0.8 collective-permute-start.1
  51.1 0.8 dynamic_slice.17
  51.9 0.8 dynamic_slice.18
  52.7 0.7 fusion.25
  53.4 3.2 %collective-permute-done.3 = bf16[1024,128]{1,0:T(8,128)(2,1)S(1)} collective-permute-done((bf16[1024,128]{1,0:T(8,128)(2,1)S(1)}, bf16[1024,128]{1,0:T(8,128)(2,1)S(1)}, u32[]{:S(2)}, u32[]{:S(2)}) %collective-permute-start.3) | collective-permute-done | bytes 262176 | tf_op jit(solution)/shard_map/ppermute | solution.py:22
  56.6 2.0 collective-permute-done.2
  58.6 8.9 %collective-permute-done.1 = bf16[1024,128]{1,0:T(8,128)(2,1)S(1)} collective-permute-done((bf16[1024,128]{1,0:T(8,128)(2,1)S(1)}, bf16[1024,128]{1,0:T(8,128)(2,1)S(1)}, u32[]{:S(2)}, u32[]{:S(2)}) %collective-permute-start.1) | collective-permute-done | bytes 262176 | tf_op jit(solution)/shard_map/ppermute | solution.py:22
  67.5 0.7 copy-done.10
  68.2 1.2 fusion.19
  69.4 1.2 pad_maximum_fusion
  70.6 62.8 %while.17 = (s32[]{:T(128)}, f32[4096,128]{1,0:T(8,128)}, f32[4096,128]{1,0:T(8,128)S(1)}, bf16[2,512,128]{2,1,0:T(8,128)(2,1)}, f32[2,512,128]{2,1,0:T(8,128)},...) while((s32[]{:T(128)}, f32[4096,128]{1,0:T(8,128)}, ...), condition=%wide.region_6.7_spmd.clone, body=%wide.region_0.6_spmd.clone.sunk | while | flops 3261858304 | bytes 230613488 | solution.py:141
  70.9 0.9 constant_dynamic-slice_fusion.5
  71.9 3.0 %fusion.90 = (f32[512]{0:T(512)S(1)}, f32[512,4096]{1,0:T(8,128)S(1)}) fusion(bf16[4096,128]{1,0:T(8,128)(2,1)} %get-tuple-element.309, bf16[2,512,128]{2,1,0:T(8,128)(2,1)} %get-tuple-element.308, s32[]{:T(128)S(6)} %copy.39, s32[512]{0:T(512)S(1)} %bitcast.129, s32[4096]{0:T(1024)S(1)} %get-tuple-element.306), kind=kOutput, calls=%fused_computation.103.clone.1 | convolution fusion | flops 545259008 | bytes 9588740 | tf_op jit(solution)/shard_map/while/body/eval_jaxpr/dot_general | solution.py:54
  74.9 1.3 fusion.91
  76.2 2.0 copy-done.1
  78.1 1.6 fusion.92
  79.8 1.6 multiply_reduce_fusion.4
  81.4 1.7 copy-done
  83.3 0.7 constant_dynamic-update-slice_fusion.2
  83.9 6.1 %convolution_add_fusion.5 = f32[4096,128]{1,0:T(8,128)S(1)} fusion(bf16[512,128]{0,1:T(8,128)(2,1)S(1)} %get-tuple-element.271, f32[4096,128]{1,0:T(8,128)S(1)} %get-tuple-element.290, f32[512,4096]{1,0:T(8,128)} %copy-done, pred[]{:T(512)S(6)} %compare.17), kind=kOutput, calls=%fused_computation.6.clone.1 | convolution fusion | flops 540016640 | bytes 12713985 | tf_op jit(solution)/shard_map/while/body/eval_jaxpr/dot_general | solution.py:75
  90.1 1.4 multiply_reduce_fusion.5
  91.6 5.6 %multiply_convert_fusion.2 = bf16[512,4096]{1,0:T(8,128)(2,1)S(1)} fusion(f32[512,4096]{1,0:T(8,128)S(1)} %get-tuple-element.272, f32[512]{0:T(512)S(1)} %get-tuple-element.273, f32[512]{0:T(512)S(1)} %fusion.91, f32[512,4096]{1,0:T(8,128)} %copy-done.1, f32[512]{0:T(512)S(1)} %get-tuple-element.265), kind=kLoop, calls=%fused_computation.clone.1 | loop fusion | flops 12582912 | bytes 20977664 | tf_op jit(solution)/shard_map/while/body/eval_jaxpr/convert_element_type | solution.py:70
  97.2 1.2 fusion.94
  98.8 2.1 convolution_add_fusion.4
  100.8 1.3 copy-done.3
  102.2 0.9 constant_dynamic-slice_fusion.5
  103.2 3.0 %fusion.90 = (f32[512]{0:T(512)S(1)}, f32[512,4096]{1,0:T(8,128)S(1)}) fusion(bf16[4096,128]{1,0:T(8,128)(2,1)} %get-tuple-element.309, bf16[2,512,128]{2,1,0:T(8,128)(2,1)} %get-tuple-element.308, s32[]{:T(128)S(6)} %copy.39, s32[512]{0:T(512)S(1)} %bitcast.129, s32[4096]{0:T(1024)S(1)} %get-tuple-element.306), kind=kOutput, calls=%fused_computation.103.clone.1 | convolution fusion | flops 545259008 | bytes 9588740 | tf_op jit(solution)/shard_map/while/body/eval_jaxpr/dot_general | solution.py:54
  106.2 1.3 fusion.91
  107.5 2.0 copy-done.1
  109.5 1.6 fusion.92
  111.1 1.6 multiply_reduce_fusion.4
  112.7 1.7 copy-done
  115.2 6.1 %convolution_add_fusion.5 = f32[4096,128]{1,0:T(8,128)S(1)} fusion(bf16[512,128]{0,1:T(8,128)(2,1)S(1)} %get-tuple-element.271, f32[4096,128]{1,0:T(8,128)S(1)} %get-tuple-element.290, f32[512,4096]{1,0:T(8,128)} %copy-done, pred[]{:T(512)S(6)} %compare.17), kind=kOutput, calls=%fused_computation.6.clone.1 | convolution fusion | flops 540016640 | bytes 12713985 | tf_op jit(solution)/shard_map/while/body/eval_jaxpr/dot_general | solution.py:75
  121.4 1.4 multiply_reduce_fusion.5
  122.9 5.6 %multiply_convert_fusion.2 = bf16[512,4096]{1,0:T(8,128)(2,1)S(1)} fusion(f32[512,4096]{1,0:T(8,128)S(1)} %get-tuple-element.272, f32[512]{0:T(512)S(1)} %get-tuple-element.273, f32[512]{0:T(512)S(1)} %fusion.91, f32[512,4096]{1,0:T(8,128)} %copy-done.1, f32[512]{0:T(512)S(1)} %get-tuple-element.265), kind=kLoop, calls=%fused_computation.clone.1 | loop fusion | flops 12582912 | bytes 20977664 | tf_op jit(solution)/shard_map/while/body/eval_jaxpr/convert_element_type | solution.py:70
  128.5 1.2 fusion.94
  130.1 2.1 convolution_add_fusion.4
  132.2 1.3 copy-done.3
  133.5 2.4 fusion.54
  136.1 1.5 collective-permute-start.6
  137.5 5.8 %collective-permute-done.4 = bf16[1024,128]{1,0:T(8,128)(2,1)S(1)} collective-permute-done((bf16[1024,128]{1,0:T(8,128)(2,1)S(1)}, bf16[1024,128]{1,0:T(8,128)(2,1)S(1)}, u32[]{:S(2)}, u32[]{:S(2)}) %collective-permute-start.4) | collective-permute-done | bytes 262176 | tf_op jit(solution)/shard_map/ppermute | solution.py:22
  143.3 1.6 collective-permute-done.6
  144.9 3.2 %collective-permute-done.5 = bf16[1024,128]{1,0:T(8,128)(2,1)S(1)} collective-permute-done((bf16[1024,128]{1,0:T(8,128)(2,1)S(1)}, bf16[1024,128]{1,0:T(8,128)(2,1)S(1)}, u32[]{:S(2)}, u32[]{:S(2)}) %collective-permute-start.5) | collective-permute-done | bytes 262176 | tf_op jit(solution)/shard_map/ppermute | solution.py:22
  149.2 2.2 reduce.2
  151.4 0.8 reshape.144
  152.2 12.7 %all-to-all-start.3 = ((bf16[128,2,512]{2,1,0:T(2,128)(2,1)}), bf16[128,2,512]{2,1,0:T(2,128)(2,1)S(1)}, u32[]{:S(2)}, u32[]{:S(2)}) async-start(bf16[128,2,512]{2,1,0:T(2,128)(2,1)} %reshape.144), calls=%async_computation.3 | async-start | bytes 524288 | tf_op jit(solution)/shard_map/all_to_all | solution.py:165
  165.4 2.2 reduce.1
  167.6 0.8 reshape.142
  168.6 9.2 %all-to-all-done.3 = bf16[128,2,512]{2,1,0:T(2,128)(2,1)S(1)} async-done(((bf16[128,2,512]{2,1,0:T(2,128)(2,1)}), bf16[128,2,512]{2,1,0:T(2,128)(2,1)S(1)}, u32[]{:S(2)}, u32[]{:S(2)}) %all-to-all-start.3) | async-done | bytes 262176 | tf_op jit(solution)/shard_map/all_to_all | solution.py:165
  177.8 6.4 %all-to-all-start.2 = ((bf16[128,2,512]{2,1,0:T(2,128)(2,1)}), bf16[128,2,512]{2,1,0:T(2,128)(2,1)S(1)}, u32[]{:S(2)}, u32[]{:S(2)}) async-start(bf16[128,2,512]{2,1,0:T(2,128)(2,1)} %reshape.142), calls=%async_computation.2 | async-start | bytes 524288 | tf_op jit(solution)/shard_map/all_to_all | solution.py:164
  185.0 1.1 fusion.31
  186.2 2.1 collective-permute-start.7
  188.4 80.1 %all-reduce.1 = (f32[4096]{0:T(1024)}, f32[4096]{0:T(1024)}) all-reduce(f32[4096]{0:T(1024)S(1)} %get-tuple-element.181, f32[4096]{0:T(1024)S(1)} %get-tuple-element.180), channel_id=1, replica_groups=mesh['seq'=128,'dp'=2] {'seq','dp'}, use_global_device_ids=true, to_apply=%region_8.9 | all-reduce | flops 8192 | bytes 65536 | tf_op jit(solution)/shard_map/psum | solution.py:177
  268.8 0.7 copy.22
  269.5 1.5 fusion.21
  (115 shorter events, 5.9 us)
Async XLA Ops:
  1.5 6.0 %collective-permute-start = (bf16[8,4096]{1,0:T(8,128)(2,1)S(1)}, bf16[8,4096]{1,0:T(8,128)(2,1)S(1)}, u32[]{:S(2)}, u32[]{:S(2)}) collective-permute-start(bf16[8,4096]{1,0:T(8,128)(2,1)S(1)} %slice_bitcast_fusion), channel_id=1, source_target_pairs={{2,0},{4,2},{6,4},{8,6},{10,8},{12,10},{14,12},{16,14},{18,16},{20... | collective-permute-start | bytes 196616 | tf_op jit(solution)/shard_map/ppermute | solution.py:16
  3.4 4.0 %copy-start.21 = (s32[32]{0:T(128)}, s32[32]{0:T(128)S(1)}, u32[]{:S(2)}) copy-start(s32[32]{0:T(128)S(1)} %get-tuple-element.165) | copy-start | bytes 388
  3.5 6.3 %copy-start.23 = (s32[32]{0:T(128)}, s32[32]{0:T(128)S(1)}, u32[]{:S(2)}) copy-start(s32[32]{0:T(128)S(1)} %get-tuple-element.166) | copy-start | bytes 388
  4.1 5.7 %copy-start.25 = (f32[32]{0:T(128)}, f32[32]{0:T(128)S(1)}, u32[]{:S(2)}) copy-start(f32[32]{0:T(128)S(1)} %fusion.52) | copy-start | bytes 388
  9.8 30.7 %all-to-all-start = ((bf16[128,8,128]{2,1,0:T(8,128)(2,1)}), bf16[128,8,128]{2,1,0:T(8,128)(2,1)S(1)}, u32[]{:S(2)}, u32[]{:S(2)}) async-start(bf16[128,8,128]{2,1,0:T(8,128)(2,1)} %bitcast.6), calls=%async_computation | async-start | bytes 524288 | tf_op jit(solution)/shard_map/all_to_all | solution.py:107
  40.5 30.1 %copy-start.5 = (bf16[128,8,128]{2,1,0:T(8,128)(2,1)}, bf16[128,8,128]{2,1,0:T(8,128)(2,1)S(1)}, u32[]{:S(2)}) copy-start(bf16[128,8,128]{2,1,0:T(8,128)(2,1)S(1)} %all-to-all-done) | copy-start | bytes 786436
  40.5 30.2 %all-to-all-start.1 = ((bf16[128,8,128]{2,1,0:T(8,128)(2,1)}), bf16[128,8,128]{2,1,0:T(8,128)(2,1)}, u32[]{:S(2)}, u32[]{:S(2)}) async-start(bf16[128,8,128]{2,1,0:T(8,128)(2,1)} %bitcast.11), calls=%async_computation.1 | async-start | bytes 524288 | tf_op jit(solution)/shard_map/all_to_all | solution.py:110
  47.8 8.9 %collective-permute-start.3 = (bf16[1024,128]{1,0:T(8,128)(2,1)S(1)}, bf16[1024,128]{1,0:T(8,128)(2,1)S(1)}, u32[]{:S(2)}, u32[]{:S(2)}) collective-permute-start(bf16[1024,128]{1,0:T(8,128)(2,1)S(1)} %bitcast.114), channel_id=1, source_target_pairs={{0,192},{2,194},{4,196},{6,198},{8,200},{10,202},{12,204},{14,206}... | collective-permute-start | bytes 786440 | tf_op jit(solution)/shard_map/ppermute | solution.py:22
  50.1 8.5 %collective-permute-start.2 = (bf16[1024,128]{1,0:T(8,128)(2,1)S(1)}, bf16[1024,128]{1,0:T(8,128)(2,1)S(1)}, u32[]{:S(2)}, u32[]{:S(2)}) collective-permute-start(bf16[1024,128]{1,0:T(8,128)(2,1)S(1)} %bitcast.115), channel_id=1, source_target_pairs={{0,128},{2,130},{4,132},{6,134},{8,136},{10,138},{12,140},{14,142}... | collective-permute-start | bytes 786440 | tf_op jit(solution)/shard_map/ppermute | solution.py:22
  50.3 17.2 %collective-permute-start.1 = (bf16[1024,128]{1,0:T(8,128)(2,1)S(1)}, bf16[1024,128]{1,0:T(8,128)(2,1)S(1)}, u32[]{:S(2)}, u32[]{:S(2)}) collective-permute-start(bf16[1024,128]{1,0:T(8,128)(2,1)S(1)} %bitcast.116), channel_id=1, source_target_pairs={{0,64},{2,66},{4,68},{6,70},{8,72},{10,74},{12,76},{14,78},{16,80}... | collective-permute-start | bytes 786440 | tf_op jit(solution)/shard_map/ppermute | solution.py:22
  51.9 18.7 %copy-start.17 = (f32[128]{0:T(128)}, f32[128]{0:T(128)S(1)}, u32[]{:S(2)}) copy-start(f32[128]{0:T(128)S(1)} %dynamic_slice.17) | copy-start | bytes 1540
  52.7 18.0 %copy-start.19 = (f32[128]{0:T(128)}, f32[128]{0:T(128)S(1)}, u32[]{:S(2)}) copy-start(f32[128]{0:T(128)S(1)} %dynamic_slice.18) | copy-start | bytes 1540
  56.6 10.9 %copy-start.8 = (bf16[1024,128]{1,0:T(8,128)(2,1)}, bf16[1024,128]{1,0:T(8,128)(2,1)S(1)}, u32[]{:S(2)}) copy-start(bf16[1024,128]{1,0:T(8,128)(2,1)S(1)} %collective-permute-done.3) | copy-start | bytes 786436
  58.6 8.9 %copy-start.9 = (bf16[1024,128]{1,0:T(8,128)(2,1)}, bf16[1024,128]{1,0:T(8,128)(2,1)S(1)}, u32[]{:S(2)}) copy-start(bf16[1024,128]{1,0:T(8,128)(2,1)S(1)} %collective-permute-done.2) | copy-start | bytes 786436
  67.5 0.7 copy-start.10
  70.6 62.8 %copy-start.20 = (f32[128]{0:T(128)S(1)}, f32[128]{0:T(128)}, u32[]{:S(2)}) copy-start(f32[128]{0:T(128)} %copy-done.19) | copy-start | bytes 1540
  70.8 4.0 %copy-start.15 = (s32[4096]{0:T(1024)}, s32[4096]{0:T(1024)S(1)}, u32[]{:S(2)}) copy-start(s32[4096]{0:T(1024)S(1)} %get-tuple-element.306) | copy-start | bytes 49156 | tf_op jit(solution)/shard_map/while
  74.9 3.3 %copy-start.1 = (f32[512,4096]{1,0:T(8,128)}, f32[512,4096]{1,0:T(8,128)S(1)}, u32[]{:S(2)}) copy-start(f32[512,4096]{1,0:T(8,128)S(1)} %get-tuple-element.264) | copy-start | bytes 25165828 | tf_op jit(solution)/shard_map/while
  79.8 3.2 %copy-start = (f32[512,4096]{1,0:T(8,128)}, f32[512,4096]{1,0:T(8,128)S(1)}, u32[]{:S(2)}) copy-start(f32[512,4096]{1,0:T(8,128)S(1)} %fusion.92) | copy-start | bytes 25165828 | tf_op jit(solution)/shard_map/while
  83.2 6.8 %slice-start = ((s8[8388608]{0:T(1024)(128)(4,1)}), s8[4194304]{0:T(1024)(128)(4,1)S(1)}, s32[]{:S(2)}) async-start(s8[8388608]{0:T(1024)(128)(4,1)} %bitcast.112), calls=%async_computation.4 | async-start | bytes 8388608 | tf_op jit(solution)/shard_map/while
  83.9 6.1 %slice-start.1 = ((s8[8388608]{0:T(1024)(128)(4,1)}), s8[4194304]{0:T(1024)(128)(4,1)S(1)}, s32[]{:S(2)}) async-start(s8[8388608]{0:T(1024)(128)(4,1)} %bitcast.112), calls=%async_computation.5 | async-start | bytes 8388608 | tf_op jit(solution)/shard_map/while
  91.5 5.6 %copy-start.4 = (bf16[4096,128]{1,0:T(8,128)(2,1)S(1)}, bf16[4096,128]{1,0:T(8,128)(2,1)}, u32[]{:S(2)}) copy-start(bf16[4096,128]{1,0:T(8,128)(2,1)} %get-tuple-element.309) | copy-start | bytes 3145732 | tf_op jit(solution)/shard_map/while
  91.5 5.6 %copy-start.11 = (f32[2,512,128]{2,1,0:T(8,128)S(1)}, f32[2,512,128]{2,1,0:T(8,128)}, u32[]{:S(2)}) copy-start(f32[2,512,128]{2,1,0:T(8,128)} %get-tuple-element.292) | copy-start | bytes 1572868 | tf_op jit(solution)/shard_map/while
  97.2 1.6 copy-start.2
  97.2 1.6 copy-start.7
  98.8 2.1 copy-start.12
  98.8 3.4 %copy-start.16 = (s32[4096]{0:T(1024)S(1)}, s32[4096]{0:T(1024)}, u32[]{:S(2)}) copy-start(s32[4096]{0:T(1024)} %copy-done.15) | copy-start | bytes 49156 | tf_op jit(solution)/shard_map/while
  100.8 1.3 copy-start.3
  102.2 4.0 %copy-start.15 = (s32[4096]{0:T(1024)}, s32[4096]{0:T(1024)S(1)}, u32[]{:S(2)}) copy-start(s32[4096]{0:T(1024)S(1)} %get-tuple-element.306) | copy-start | bytes 49156 | tf_op jit(solution)/shard_map/while
  106.2 3.3 %copy-start.1 = (f32[512,4096]{1,0:T(8,128)}, f32[512,4096]{1,0:T(8,128)S(1)}, u32[]{:S(2)}) copy-start(f32[512,4096]{1,0:T(8,128)S(1)} %get-tuple-element.264) | copy-start | bytes 25165828 | tf_op jit(solution)/shard_map/while
  111.1 3.2 %copy-start = (f32[512,4096]{1,0:T(8,128)}, f32[512,4096]{1,0:T(8,128)S(1)}, u32[]{:S(2)}) copy-start(f32[512,4096]{1,0:T(8,128)S(1)} %fusion.92) | copy-start | bytes 25165828 | tf_op jit(solution)/shard_map/while
  114.6 6.8 %slice-start = ((s8[8388608]{0:T(1024)(128)(4,1)}), s8[4194304]{0:T(1024)(128)(4,1)S(1)}, s32[]{:S(2)}) async-start(s8[8388608]{0:T(1024)(128)(4,1)} %bitcast.112), calls=%async_computation.4 | async-start | bytes 8388608 | tf_op jit(solution)/shard_map/while
  115.2 6.1 %slice-start.1 = ((s8[8388608]{0:T(1024)(128)(4,1)}), s8[4194304]{0:T(1024)(128)(4,1)S(1)}, s32[]{:S(2)}) async-start(s8[8388608]{0:T(1024)(128)(4,1)} %bitcast.112), calls=%async_computation.5 | async-start | bytes 8388608 | tf_op jit(solution)/shard_map/while
  122.9 5.6 %copy-start.4 = (bf16[4096,128]{1,0:T(8,128)(2,1)S(1)}, bf16[4096,128]{1,0:T(8,128)(2,1)}, u32[]{:S(2)}) copy-start(bf16[4096,128]{1,0:T(8,128)(2,1)} %get-tuple-element.309) | copy-start | bytes 3145732 | tf_op jit(solution)/shard_map/while
  122.9 5.6 %copy-start.11 = (f32[2,512,128]{2,1,0:T(8,128)S(1)}, f32[2,512,128]{2,1,0:T(8,128)}, u32[]{:S(2)}) copy-start(f32[2,512,128]{2,1,0:T(8,128)} %get-tuple-element.292) | copy-start | bytes 1572868 | tf_op jit(solution)/shard_map/while
  128.5 1.6 copy-start.2
  128.5 1.6 copy-start.7
  130.1 2.1 copy-start.12
  130.1 3.4 %copy-start.16 = (s32[4096]{0:T(1024)S(1)}, s32[4096]{0:T(1024)}, u32[]{:S(2)}) copy-start(s32[4096]{0:T(1024)} %copy-done.15) | copy-start | bytes 49156 | tf_op jit(solution)/shard_map/while
  132.1 1.3 copy-start.3
  133.5 14.6 %copy-start.13 = (f32[2,512,128]{2,1,0:T(8,128)S(1)}, f32[2,512,128]{2,1,0:T(8,128)}, u32[]{:S(2)}) copy-start(f32[2,512,128]{2,1,0:T(8,128)} %get-tuple-element.65) | copy-start | bytes 1572868
  133.5 14.6 %copy-start.18 = (f32[128]{0:T(128)S(1)}, f32[128]{0:T(128)}, u32[]{:S(2)}) copy-start(f32[128]{0:T(128)} %copy-done.17) | copy-start | bytes 1540
  136.0 7.3 %collective-permute-start.4 = (bf16[1024,128]{1,0:T(8,128)(2,1)S(1)}, bf16[1024,128]{1,0:T(8,128)(2,1)S(1)}, u32[]{:S(2)}, u32[]{:S(2)}) collective-permute-start(bf16[1024,128]{1,0:T(8,128)(2,1)S(1)} %get-tuple-element.177), channel_id=1, source_target_pairs={{0,192},{2,194},{4,196},{6,198},{8,200},{10,202},{12,204},{14,206}... | collective-permute-start | bytes 786440 | tf_op jit(solution)/shard_map/ppermute | solution.py:22
  136.1 8.8 %collective-permute-start.6 = (bf16[1024,128]{1,0:T(8,128)(2,1)S(1)}, bf16[1024,128]{1,0:T(8,128)(2,1)S(1)}, u32[]{:S(2)}, u32[]{:S(2)}) collective-permute-start(bf16[1024,128]{1,0:T(8,128)(2,1)S(1)} %get-tuple-element.178), channel_id=1, source_target_pairs={{0,64},{2,66},{4,68},{6,70},{8,72},{10,74},{12,76},{14,78},{16,80}... | collective-permute-start | bytes 786440 | tf_op jit(solution)/shard_map/ppermute | solution.py:22
  137.5 10.5 %collective-permute-start.5 = (bf16[1024,128]{1,0:T(8,128)(2,1)S(1)}, bf16[1024,128]{1,0:T(8,128)(2,1)S(1)}, u32[]{:S(2)}, u32[]{:S(2)}) collective-permute-start(bf16[1024,128]{1,0:T(8,128)(2,1)S(1)} %get-tuple-element.179), channel_id=1, source_target_pairs={{0,128},{2,130},{4,132},{6,134},{8,136},{10,138},{12,140},{14,142}... | collective-permute-start | bytes 786440 | tf_op jit(solution)/shard_map/ppermute | solution.py:22
  148.1 16.9 %copy-start.14 = (bf16[2,512,128]{2,1,0:T(8,128)(2,1)S(1)}, bf16[2,512,128]{2,1,0:T(8,128)(2,1)}, u32[]{:S(2)}) copy-start(bf16[2,512,128]{2,1,0:T(8,128)(2,1)} %get-tuple-element.64) | copy-start | bytes 786436
  148.7 19.8 %copy-start.6 = (bf16[128,8,128]{2,1,0:T(8,128)(2,1)S(1)}, bf16[128,8,128]{2,1,0:T(8,128)(2,1)}, u32[]{:S(2)}) copy-start(bf16[128,8,128]{2,1,0:T(8,128)(2,1)} %copy-done.5) | copy-start | bytes 786436
  152.2 25.6 %all-to-all-start.3 = ((bf16[128,2,512]{2,1,0:T(2,128)(2,1)}), bf16[128,2,512]{2,1,0:T(2,128)(2,1)S(1)}, u32[]{:S(2)}, u32[]{:S(2)}) async-start(bf16[128,2,512]{2,1,0:T(2,128)(2,1)} %reshape.144), calls=%async_computation.3 | async-start | bytes 524288 | tf_op jit(solution)/shard_map/all_to_all | solution.py:165
  165.4 19.6 %copy-start.22 = (s32[32]{0:T(128)S(1)}, s32[32]{0:T(128)}, u32[]{:S(2)}) copy-start(s32[32]{0:T(128)} %copy-done.21) | copy-start | bytes 388
  165.4 19.6 %copy-start.24 = (s32[32]{0:T(128)S(1)}, s32[32]{0:T(128)}, u32[]{:S(2)}) copy-start(s32[32]{0:T(128)} %copy-done.23) | copy-start | bytes 388
  165.4 19.6 %copy-start.26 = (f32[32]{0:T(128)S(1)}, f32[32]{0:T(128)}, u32[]{:S(2)}) copy-start(f32[32]{0:T(128)} %copy-done.25) | copy-start | bytes 388
  177.8 90.8 %all-to-all-start.2 = ((bf16[128,2,512]{2,1,0:T(2,128)(2,1)}), bf16[128,2,512]{2,1,0:T(2,128)(2,1)S(1)}, u32[]{:S(2)}, u32[]{:S(2)}) async-start(bf16[128,2,512]{2,1,0:T(2,128)(2,1)} %reshape.142), calls=%async_computation.2 | async-start | bytes 524288 | tf_op jit(solution)/shard_map/all_to_all | solution.py:164
  186.2 83.3 %collective-permute-start.7 = (bf16[8,4096]{1,0:T(8,128)(2,1)S(1)}, bf16[8,4096]{1,0:T(8,128)(2,1)S(1)}, u32[]{:S(2)}, u32[]{:S(2)}) collective-permute-start(bf16[8,4096]{1,0:T(8,128)(2,1)S(1)} %slice.56), channel_id=1, source_target_pairs={{0,2},{2,4},{4,6},{6,8},{8,10},{10,12},{12,14},{14,16},{16,18},{18... | collective-permute-start | bytes 196616 | tf_op jit(solution)/shard_map/ppermute | solution.py:16
where the time goes:
time: 272 us; the launch traced here: 271 us
  blocking collectives  80.1 us (29%)
  starting transfers between devices  52.6 us (19%)
  waiting for transfers between devices  49.8 us (18%)
  matrix products  34.2 us (13%)
  other arithmetic  31 us (11%)
  local copies, waits for them, and re-layouts  21.6 us (8%)
    psum x1, blocking collectives, on_device(): grad_qgain, grad_kgain = lax.psum((qgain_vec, kgain_vec), ('seq', 'dp'))  80.1 us
    ppermute x6, waiting for transfers between devices, from_behind(): return lax.ppermute(value, axis, pairs)  24.6 us
    all_to_all x1, starting transfers between devices, on_device(): lax.all_to_all(to_heads_layout(pooled, heads, width), 'seq', split_axis=0...  17.9 us
    all_to_all x1, starting transfers between devices, on_device(): lax.all_to_all(as_sent(dpooled_h[None]), 'seq', split_axis=1, concat_axis...  12.7 us
    all_to_all x1, waiting for transfers between devices, on_device(): lax.all_to_all(to_heads_layout(pooled, heads, width), 'seq', split_axis=0...  12.6 us
    dot_general x2, matrix products, attend_block(): lax.dot_general(weights, dmixed_b, (((0,), (0,)), ((), ())), preferred_el...  12.3 us
    convert_element_type x2, other arithmetic, attend_block(): dscaled = (dscores * scale).astype(jnp.bfloat16)  11.1 us
    while x48, local copies, waits for them, and re-layouts  10.6 us
  transfers between devices with their start and end apart: 12, of which 9 were waited for; matrix products, arithmetic and copies ran while one was open for 5% of the time, Pallas kernels for 0%

commit v1 on v0

v1 whole, which is shorter than its diff:
```python
import functools
import math

import jax
import jax.numpy as jnp
from jax import lax
from jax.experimental import pallas as pl
from jax.experimental.pallas import tpu as pltpu
from jax.sharding import PartitionSpec as P

f32 = jnp.float32
bf16 = jnp.bfloat16
HEAD_DIM = 128
HEADS = 32
PIECE = 32
BLOCK = 512
EPS = 1e-6
NT = (((1,), (1,)), ((), ()))
TN = (((0,), (0,)), ((), ()))


def place():
    seq = lax.axis_index("seq")
    core = lax.axis_index("dp")
    y = seq // 32
    return seq, core, y, (seq // 8) % 4, seq % 8


def at(seq, core):
    return {"seq": seq, "dp": core}


def low_block(y, core):
    return core + 2 * (((y + 1) // 2) % 2)


def owner(y, x, doc):
    block = 2 * y + x // 2
    high = block // 4
    low = block + high * (7 - 2 * block)
    half = low // 2
    return (doc * (3 - half) + (1 - doc) * half), low % 2, high


def source(y, core, i):
    low = low_block(y, core)
    high = i // 16
    block = low + high * (7 - 2 * low)
    return block * 16 + i % 16, y // 2, i * PIECE


def head_at(x, z, i):
    return ((x + i // 8) % 4) * 8 + (z + i % 8) % 8


MESH = pl.DeviceIdType.MESH


def signal(sem, seq, core):
    pl.semaphore_signal(sem, inc=1, device_id=at(seq, core), device_id_type=MESH)


def remote(src, dst, send, recv, seq, core):
    return pltpu.make_async_remote_copy(
        src_ref=src, dst_ref=dst, send_sem=send, recv_sem=recv,
        device_id=at(seq, core), device_id_type=MESH,
    )


def column(row, count):
    r = lax.broadcasted_iota(jnp.int32, (count, count), 0)
    c = lax.broadcasted_iota(jnp.int32, (count, count), 1)
    return jnp.sum(jnp.where(r == c, jnp.broadcast_to(row, (count, count)), 0), 1, keepdims=True)


def dispatch(bytes_ref, starts, lengths, cot, kfull, cot_h, pooled, sums, spill, spill_in,
             s_spill, r_spill, s_pool, r_pool, s_cot, r_cot, s_key, r_key):
    seq, core, y, x, z = place()
    oy, ocore, ohigh = owner(y, x, core)
    mine = (oy == y) & (ocore == core)
    low = low_block(y, core)
    partner = seq + 32 - 64 * (y % 2)
    before = (seq + 127) % 128
    after = (seq + 1) % 128

    barrier = pltpu.get_barrier_semaphore()

    def greet(i, _):
        s, d, _row = source(y, core, i)

        @pl.when((s != seq) | (d != core))
        def _():
            signal(barrier, s, d)

        return 0

    lax.fori_loop(0, 32, greet, 0)
    signal(barrier, seq, 1 - core)
    signal(barrier, partner, core)
    signal(barrier, after, core)

    base = seq * 128
    start = column(starts[...], PIECE) - base
    length = column(lengths[...], PIECE)
    at_byte = lax.broadcasted_iota(jnp.int32, (PIECE, 128), 1)
    member = ((at_byte >= start) & (at_byte < start + length)).astype(f32).astype(bf16)
    first = starts[:, 0:1] - base
    lead = (lax.broadcasted_iota(jnp.int32, (16, 128), 1) < first).astype(f32).astype(bf16)
    spill[...] = jnp.dot(lead, bytes_ref[...], preferred_element_type=f32)[0:1, :]

    @pl.when(mine)
    def _():
        pl.semaphore_wait(barrier, 34)

    @pl.when(jnp.logical_not(mine))
    def _():
        pl.semaphore_wait(barrier, 35)

    spilling = remote(spill, spill_in, s_spill, r_spill, before, core)
    spilling.start()
    sums[...] = jnp.dot(member, bytes_ref[...], preferred_element_type=f32)
    inverse = 1.0 / length.astype(f32)
    spilling.wait_recv()
    last = (lax.broadcasted_iota(jnp.int32, (PIECE, 1), 0) == PIECE - 1) & (seq < 127)
    pooled[...] = ((sums[...] + jnp.where(last, spill_in[...], 0.0)) * inverse).astype(bf16)

    krow = pl.multiple_of(seq * PIECE, PIECE)
    crow = pl.multiple_of(ohigh * BLOCK + (seq % 16) * PIECE, PIECE)

    def scatter(src, dst, row, send, recv):
        def step(i, _):
            h = head_at(x, z, i)
            part = src.at[:, pl.ds(pl.multiple_of(h * HEAD_DIM, HEAD_DIM), HEAD_DIM)]
            there = dst.at[pl.ds(row, PIECE), :]
            target = oy * 32 + h
            local = (target == seq) & (ocore == core)

            @pl.when(local)
            def _():
                pltpu.make_async_copy(part, there, recv).start()

            @pl.when(jnp.logical_not(local))
            def _():
                remote(part, there, send, recv, target, ocore).start()

            return 0

        lax.fori_loop(0, 32, step, 0)

    scatter(pooled, kfull, krow, s_pool, r_pool)
    scatter(cot, cot_h, crow, s_cot, r_cot)

    def rows(block):
        return kfull.at[pl.ds(pl.multiple_of(block * BLOCK, BLOCK), BLOCK), :]

    pltpu.make_async_copy(kfull.at[pl.ds(0, 1024), :], kfull.at[pl.ds(0, 1024), :], r_pool).wait()
    copies = []
    for i, block in enumerate((low, 7 - low)):
        a = remote(rows(block), rows(block), s_key.at[i], r_key.at[i], partner, core)
        b = remote(rows(block), rows(block), s_key.at[2 + i], r_key.at[2 + i], seq, 1 - core)
        a.start()
        b.start()
        copies.append((a, b))
    far = low + 2 - 4 * (low // 2)
    for i, block in enumerate((far, 7 - far)):
        copies[i][0].wait_recv()
        c = remote(rows(block), rows(block), s_key.at[4 + i], r_key.at[4 + i], seq, 1 - core)
        c.start()
        copies[i] = copies[i] + (c,)
    for a, b, c in copies:
        b.wait_recv()
        c.wait_recv()
        a.wait_send()
        b.wait_send()
        c.wait_send()
    pltpu.make_async_copy(cot_h, cot_h, r_cot).wait()
    spilling.wait_send()

    @pl.when(mine)
    def _():
        for src, sem in ((pooled, s_pool), (cot, s_cot)):
            part = src.at[:, pl.ds(0, 31 * HEAD_DIM)]
            pltpu.make_async_copy(part, part, sem).wait()

    @pl.when(jnp.logical_not(mine))
    def _():
        for src, sem in ((pooled, s_pool), (cot, s_cot)):
            pltpu.make_async_copy(src, src, sem).wait()


def give_back(starts, lengths, out_h, side, gains, patch_out, grad, gq, gk,
              to_sib, from_sib, to_far, from_far, mine_b, dpool, spill, spill_in, column_in, plane,
              s_out, r_out, s_sib, r_sib, s_far, r_far, s_dp, r_dp, s_col, r_col, s_pla, r_pla,
              s_spill, r_spill):
    seq, core, y, x, z = place()
    oy, ocore, ohigh = owner(y, x, core)
    mine = (oy == y) & (ocore == core)
    low = low_block(y, core)
    partner = seq + 32 - 64 * (y % 2)
    before = (seq + 127) % 128
    after = (seq + 1) % 128
    head = x * 8 + z

    barrier = pltpu.get_barrier_semaphore()

    def greet(i, _):
        h = head_at(x, z, i)
        target = oy * 32 + h

        @pl.when((target != seq) | (ocore != core))
        def _():
            signal(barrier, target, ocore)

        return 0

    lax.fori_loop(0, 32, greet, 0)

    def greet_plane(i, _):
        signal(barrier, y * 32 + head_at(x, z, i), core)
        return 0

    lax.fori_loop(1, 32, greet_plane, 0)

    def greet_column(i, _):
        c = (y * 2 + core + i) % 8
        signal(barrier, (c // 2) * 32 + head, c % 2)
        return 0

    lax.fori_loop(1, 8, greet_column, 0)
    signal(barrier, seq, 1 - core)
    signal(barrier, partner, core)
    signal(barrier, before, core)

    def rows(block):
        return pl.ds(pl.multiple_of(block * BLOCK, BLOCK), BLOCK)

    sib = low + 1 - 2 * (low % 2)
    far = low + 2 - 4 * (low // 2)
    farsib = sib + 2 - 4 * (sib // 2)
    for i, block in enumerate((farsib, 7 - farsib, sib, 7 - sib)):
        to_sib[i * BLOCK:(i + 1) * BLOCK, :] = side[rows(block), :].astype(bf16)
    column_in[pl.ds(y * 2 + core, 1)] = gains[...][None]

    @pl.when(mine)
    def _():
        pl.semaphore_wait(barrier, 31 + 31 + 7 + 3)

    @pl.when(jnp.logical_not(mine))
    def _():
        pl.semaphore_wait(barrier, 32 + 31 + 7 + 3)

    sib_a = remote(to_sib.at[0:1024], from_sib.at[0:1024], s_sib.at[0], r_sib.at[0], seq, 1 - core)
    sib_b = remote(to_sib.at[1024:2048], from_sib.at[1024:2048], s_sib.at[1], r_sib.at[1], seq, 1 - core)
    sib_a.start()
    sib_b.start()

    def send_column(i, _):
        c = (y * 2 + core + i) % 8
        slot = column_in.at[pl.ds(y * 2 + core, 1)]
        remote(slot, slot, s_col, r_col, (c // 2) * 32 + head, c % 2).start()
        return 0

    lax.fori_loop(1, 8, send_column, 0)

    column_of = pl.ds(pl.multiple_of(head * HEAD_DIM, HEAD_DIM), HEAD_DIM)

    def scatter(src, dst, send, recv):
        def step(i, _):
            j = (i + head) % 32
            s, d, row = source(y, core, j)
            part = src.at[pl.ds(pl.multiple_of(row, PIECE), PIECE), :]
            there = dst.at[:, column_of]
            local = (s == seq) & (d == core)

            @pl.when(local)
            def _():
                pltpu.make_async_copy(part, there, recv).start()

            @pl.when(jnp.logical_not(local))
            def _():
                remote(part, there, send, recv, s, d).start()

            return 0

        lax.fori_loop(0, 32, step, 0)

    sib_a.wait_recv()
    for i, block in enumerate((far, 7 - far)):
        half = pl.ds(i * BLOCK, BLOCK)
        to_far[half, :] = (side[rows(block), :] + from_sib[half, :].astype(f32)).astype(bf16)
    across = remote(to_far, from_far, s_far, r_far, partner, core)
    across.start()
    scatter(out_h, patch_out, s_out, r_out)

    pltpu.make_async_copy(column_in.at[0:7], column_in.at[0:7], r_col).wait()
    total = column_in[0]
    for i in range(1, 8):
        total = total + column_in[i]
    plane[pl.ds(head, 1)] = total[None]

    def send_plane(i, _):
        slot = plane.at[pl.ds(head, 1)]
        remote(slot, slot, s_pla, r_pla, y * 32 + head_at(x, z, i), core).start()
        return 0

    lax.fori_loop(1, 32, send_plane, 0)

    sib_b.wait_recv()
    across.wait_recv()
    for i, block in enumerate((low, 7 - low)):
        half = pl.ds(i * BLOCK, BLOCK)
        mine_b[half, :] = (
            side[rows(block), :]
            + from_sib[1024 + i * BLOCK:1024 + (i + 1) * BLOCK, :].astype(f32)
            + from_far[half, :].astype(f32)
        ).astype(bf16)
    scatter(mine_b, dpool, s_dp, r_dp)

    base = seq * 128
    start = starts[...] - base
    length = lengths[...]
    at_byte = lax.broadcasted_iota(jnp.int32, (128, PIECE), 0)
    inside = (at_byte >= start) & (at_byte < start + length)
    member = inside.astype(f32).astype(bf16)
    inverse = 1.0 / length.astype(f32)
    by_byte = jnp.sum(jnp.where(inside, inverse, 0.0), 1, keepdims=True)
    lead = lax.broadcasted_iota(jnp.int32, (128, 1), 0) < start[:, 0:1]

    pltpu.make_async_copy(plane.at[0:31], plane.at[0:31], r_pla).wait()
    for i in range(HEADS):
        gq[i:i + 1, :] = plane[i, 0:1, :]
        gk[i:i + 1, :] = plane[i, 1:2, :]

    pltpu.make_async_copy(dpool, dpool, r_dp).wait()
    spill[...] = dpool[16:32, :].astype(f32)[15:16, :] * inverse[:, PIECE - 1:PIECE]
    spilling = remote(spill, spill_in, s_spill, r_spill, after, core)
    spilling.start()
    grad[...] = jnp.dot(member, dpool[...], preferred_element_type=f32) * by_byte
    spilling.wait_recv()
    grad[0:8, :] = jnp.where(lead[0:8, :], spill_in[...], grad[0:8, :])

    pltpu.make_async_copy(patch_out, patch_out, r_out).wait()
    spilling.wait_send()
    sib_a.wait_send()
    sib_b.wait_send()
    across.wait_send()
    pltpu.make_async_copy(column_in.at[0:7], column_in.at[0:7], s_col).wait()
    pltpu.make_async_copy(plane.at[0:31], plane.at[0:31], s_pla).wait()

    @pl.when(mine)
    def _():
        for src, sem in ((out_h, s_out), (mine_b, s_dp)):
            part = src.at[0:31 * PIECE]
            pltpu.make_async_copy(part, part, sem).wait()

    @pl.when(jnp.logical_not(mine))
    def _():
        for src, sem in ((out_h, s_out), (mine_b, s_dp)):
            pltpu.make_async_copy(src, src, sem).wait()


SCALE=HEAD_DIM**-0.5
C2=SCALE*math.log2(math.e)

def lanes(x, op):
    acc = x[:, :128]
    for i in range(1, x.shape[1]//128):
        acc = op(acc, x[:, i*128:(i+1)*128])
    return acc

def attend(blk, first, kfull, keyed, cot, cot_row, out, s_ref, w_ref, d_ref, dk, dv, dq_ref, qgain):
    row0 = pl.multiple_of(blk * BLOCK, BLOCK)
    q = (kfull[pl.ds(row0, BLOCK), :].astype(f32) * qgain).astype(bf16)
    def rows(j): return pl.ds(pl.multiple_of(j * BLOCK, BLOCK), BLOCK)
    def scores(j, m, diag):
        s = lax.dot_general(q, keyed[rows(j), :], NT, preferred_element_type=f32)
        if diag:
            r = lax.broadcasted_iota(jnp.int32, s.shape, 0); c = lax.broadcasted_iota(jnp.int32, s.shape, 1)
            s = jnp.where(c <= r, s, -1e30)
        s_ref[:, rows(j)] = s
        return jnp.maximum(m, lanes(s, jnp.maximum))
    m = lax.fori_loop(0, blk, lambda j, m: scores(j, m, False), jnp.full((BLOCK, 128), -1e30, f32))
    m = scores(blk, m, True)
    top = jnp.max(m, -1, keepdims=True)
    def expo(j, l):
        e = jnp.exp2((s_ref[:, rows(j)] - top) * C2)
        s_ref[:, rows(j)] = e
        return l + lanes(e, jnp.add)
    l = lax.fori_loop(0, blk + 1, expo, jnp.zeros((BLOCK, 128), f32))
    inv = 1.0 / jnp.sum(l, -1, keepdims=True)
    def mix(j, acc):
        w = (s_ref[:, rows(j)] * inv).astype(bf16)
        w_ref[:, rows(j)] = w
        return acc + jnp.dot(w, kfull[rows(j), :], preferred_element_type=f32)
    mixed = lax.fori_loop(0, blk + 1, mix, jnp.zeros((BLOCK, 128), f32))
    spread = jnp.sqrt(jnp.mean(mixed * mixed, -1, keepdims=True) + EPS)
    rs = 1.0 / spread
    out[cot_row:cot_row+BLOCK, :] = (mixed * rs).astype(bf16)
    g = cot[cot_row:cot_row+BLOCK, :].astype(f32)
    dm = g * rs - mixed * (jnp.sum(g * mixed, -1, keepdims=True) * (rs * rs * rs) * (1.0 / HEAD_DIM))
    dmb = dm.astype(bf16)
    def dprob(j, r):
        dp = lax.dot_general(dmb, kfull[rows(j), :], NT, preferred_element_type=f32)
        d_ref[:, rows(j)] = dp
        v = lax.dot_general(w_ref[:, rows(j)], dmb, TN, preferred_element_type=f32)
        if first: dv[rows(j), :] = v
        else: dv[rows(j), :] += v
        return r + lanes(dp * s_ref[:, rows(j)], jnp.add)
    r = lax.fori_loop(0, blk + 1, dprob, jnp.zeros((BLOCK, 128), f32))
    r = jnp.sum(r, -1, keepdims=True) * inv
    invs = inv * SCALE
    def back(j, acc):
        ds = ((s_ref[:, rows(j)] * invs) * (d_ref[:, rows(j)] - r)).astype(bf16)
        k = lax.dot_general(ds, q, TN, preferred_element_type=f32)
        if first: dk[rows(j), :] = k
        else: dk[rows(j), :] += k
        return acc + jnp.dot(ds, keyed[rows(j), :], preferred_element_type=f32)
    dq_ref[...] = lax.fori_loop(0, blk + 1, back, jnp.zeros((BLOCK, 128), f32))

def attn_body(lo, kfull, cot, qgain, kgain, out, side, gains, keyed, s_ref, w_ref, d_ref, dk, dv, dq_ref):
    hi = 7 - lo
    def chunk(j): return pl.ds(pl.multiple_of(j * BLOCK, BLOCK), BLOCK)
    def prep(j, _):
        keyed[chunk(j), :] = (kfull[chunk(j), :].astype(f32) * kgain).astype(bf16)
        return 0
    lax.fori_loop(0, hi + 1, prep, 0)
    def clear(j, _):
        dk[chunk(j), :] = jnp.zeros((BLOCK, 128), f32)
        dv[chunk(j), :] = jnp.zeros((BLOCK, 128), f32)
        return 0
    lax.fori_loop(hi + 1, 8, clear, 0)
    attend(hi, True, kfull, keyed, cot, BLOCK, out, s_ref, w_ref, d_ref, dk, dv, dq_ref.at[1], qgain)
    attend(lo, False, kfull, keyed, cot, 0, out, s_ref, w_ref, d_ref, dk, dv, dq_ref.at[0], qgain)
    def finish(j, acc):
        d = dk[chunk(j), :]
        side[chunk(j), :] = d * kgain + dv[chunk(j), :]
        return acc + jnp.sum(d * kfull[chunk(j), :].astype(f32), 0, keepdims=True)
    gk = lax.fori_loop(0, 8, finish, jnp.zeros((1, 128), f32))
    gq = jnp.zeros((1, 128), f32)
    for i, b in ((0, lo), (1, hi)):
        dq = dq_ref[i]
        side[chunk(b), :] += dq * qgain
        gq = gq + jnp.sum(dq * kfull[chunk(b), :].astype(f32), 0, keepdims=True)
    gains[0:1, :] = gq
    gains[1:2, :] = gk


def attn_scratch():
    return [pltpu.VMEM((4096, HEAD_DIM), bf16), pltpu.VMEM((BLOCK, 4096), f32), pltpu.VMEM((BLOCK, 4096), bf16),
            pltpu.VMEM((BLOCK, 4096), f32), pltpu.VMEM((4096, HEAD_DIM), f32), pltpu.VMEM((4096, HEAD_DIM), f32),
            pltpu.VMEM((2, BLOCK, HEAD_DIM), f32)]


VMEM = pl.BlockSpec(memory_space=pltpu.VMEM)
DMA = pltpu.SemaphoreType.DMA


def shape(dims, dtype):
    return jax.ShapeDtypeStruct(dims, dtype)


def attend_kernel(kfull, cot, qgain, kgain, out, side, gains, *scratch):
    seq, core, y, x, z = place()
    head = x * 8 + z
    attn_body(low_block(y, core), kfull, cot, qgain[pl.ds(head, 1), :], kgain[pl.ds(head, 1), :],
              out, side, gains, *scratch)


def on_device(byte_states, patch_starts, patch_lengths, query_gain, key_gain, out_cotangent):
    states = byte_states[0]
    cot = out_cotangent[0]
    width = states.shape[1]
    kfull, cot_h = pl.pallas_call(
        dispatch,
        out_shape=(shape((4096, HEAD_DIM), bf16), shape((1024, HEAD_DIM), bf16)),
        in_specs=[VMEM] * 4,
        out_specs=(VMEM, VMEM),
        scratch_shapes=[
            pltpu.VMEM((PIECE, width), bf16),
            pltpu.VMEM((PIECE, width), f32),
            pltpu.VMEM((1, width), f32),
            pltpu.VMEM((1, width), f32),
            DMA, DMA, DMA, DMA, DMA, DMA, DMA((6,)), DMA((6,)),
        ],
        compiler_params=pltpu.CompilerParams(
            collective_id=0, has_side_effects=True, vmem_limit_bytes=40 << 20
        ),
    )(states, patch_starts, patch_lengths, cot)
    out_h, side, gains = pl.pallas_call(
        attend_kernel,
        out_shape=(shape((1024, HEAD_DIM), bf16), shape((4096, HEAD_DIM), f32), shape((2, HEAD_DIM), f32)),
        in_specs=[VMEM] * 4,
        out_specs=(VMEM,) * 3,
        scratch_shapes=attn_scratch(),
        compiler_params=pltpu.CompilerParams(vmem_limit_bytes=56 << 20),
    )(kfull, cot_h, query_gain.reshape(HEADS, HEAD_DIM), key_gain.reshape(HEADS, HEAD_DIM))
    patch_out, grad, gq, gk = pl.pallas_call(
        give_back,
        out_shape=(shape((PIECE, width), bf16), shape((128, width), f32),
                   shape((HEADS, HEAD_DIM), f32), shape((HEADS, HEAD_DIM), f32)),
        in_specs=[VMEM] * 5,
        out_specs=(VMEM,) * 4,
        scratch_shapes=[
            pltpu.VMEM((2048, HEAD_DIM), bf16),
            pltpu.VMEM((2048, HEAD_DIM), bf16),
            pltpu.VMEM((1024, HEAD_DIM), bf16),
            pltpu.VMEM((1024, HEAD_DIM), bf16),
            pltpu.VMEM((1024, HEAD_DIM), bf16),
            pltpu.VMEM((PIECE, width), bf16),
            pltpu.VMEM((1, width), f32),
            pltpu.VMEM((1, width), f32),
            pltpu.VMEM((8, 2, HEAD_DIM), f32),
            pltpu.VMEM((HEADS, 2, HEAD_DIM), f32),
            DMA, DMA, DMA((2,)), DMA((2,)), DMA, DMA, DMA, DMA, DMA, DMA, DMA, DMA, DMA, DMA,
        ],
        compiler_params=pltpu.CompilerParams(
            collective_id=1, has_side_effects=True, vmem_limit_bytes=48 << 20
        ),
    )(patch_starts, patch_lengths, out_h, side, gains)
    return patch_out[None], grad[None], gq.reshape(width), gk.reshape(width)


def solution(mesh):
    rows = P("dp", "seq", None)
    flat = P("dp", "seq")
    return jax.shard_map(
        on_device,
        mesh=mesh,
        in_specs=(rows, flat, flat, P(), P(), rows),
        out_specs=(rows, rows, P(), P()),
        check_vma=False,
    )
```

time: 272 us -> 98.9 us (0.36)
  Pallas kernels: 0 us -> 86.3 us
  blocking collectives: 80.1 us -> 0 us
  starting transfers between devices: 52.6 us -> 0 us
  waiting for transfers between devices: 49.8 us -> 0 us
  matrix products: 34.2 us -> 0 us
  other arithmetic: 31 us -> 0 us
  local copies, waits for them, and re-layouts: 21.6 us -> 11.6 us
    pallas_call x0 -> x3, Pallas kernels: none -> 86.3 us  [the longest x1 32.9 us: on_device(): pl.pallas_call(dispatch, out_shape=(shape((4096, HEAD_DIM), bf16), shape(...]
    psum x1 -> x0, blocking collectives: 80.1 us -> none  [on_device(): grad_qgain, grad_kgain = lax.psum((qgain_vec, kgain_vec), ('seq', 'dp'))]
    all_to_all x4 -> x0, starting transfers between devices: 44.4 us -> none  [the longest x1 17.9 us: on_device(): lax.all_to_all(to_heads_layout(pooled, heads, width), 'seq', split_axis=0...]
    dot_general x14 -> x0, matrix products: 34.2 us -> none  [the longest x2 12.3 us: attend_block(): lax.dot_general(weights, dmixed_b, (((0,), (0,)), ((), ())), preferred_el...]
    ppermute x8 -> x0, waiting for transfers between devices: 28 us -> none  [the longest x6 24.6 us: from_behind(): return lax.ppermute(value, axis, pairs)]
    all_to_all x4 -> x0, waiting for transfers between devices: 21.8 us -> none  [the longest x1 12.6 us: on_device(): lax.all_to_all(to_heads_layout(pooled, heads, width), 'seq', split_axis=0...]
    convert_element_type x7 -> x0, other arithmetic: 13.8 us -> none  [the longest x2 11.1 us: attend_block(): dscaled = (dscores * scale).astype(jnp.bfloat16)]
    while x48 -> x0, local copies, waits for them, and re-layouts: 10.6 us -> none
  transfers between devices with their start and end apart: 12 -> 0, of which waited for: 9 -> 0; matrix products, arithmetic and copies ran while one was open for 5% -> 0% of each run, Pallas kernels for 0% -> 0%
where the time goes in v1:
time: 98.9 us; the launch traced here: 98.7 us
  Pallas kernels  86.3 us (87%)
  local copies, waits for them, and re-layouts  11.6 us (12%)
    pallas_call x1, Pallas kernels, on_device(): pl.pallas_call(dispatch, out_shape=(shape((4096, HEAD_DIM), bf16), shape(...  32.9 us
    pallas_call x1, Pallas kernels, on_device(): pl.pallas_call(give_back, out_shape=(shape((PIECE, width), bf16), shape((...  31.2 us
    pallas_call x1, Pallas kernels, on_device(): pl.pallas_call(attend_kernel, out_shape=(shape((1024, HEAD_DIM), bf16), s...  22.3 us
    unnamed x26, local copies, waits for them, and re-layouts  11.6 us

profile of v1, /device:TPU:1, one launch (start us, length us, event | category | flops | bytes accessed | tf_op | source)
XLA Modules:
  0.0 98.7 jit_solution(4908857516487441453)
XLA Ops:
  0.6 0.0 copy-start.9
  0.6 0.0 copy-start.7
  0.7 0.0 copy-start.1
  0.7 1.2 %copy-done.1 = bf16[1,128,4096]{2,1,0:T(8,128)(2,1)S(1)} copy-done((bf16[1,128,4096]{2,1,0:T(8,128)(2,1)S(1)}, bf16[1,128,4096]{2,1,0:T(8,128)(2,1)}, u32[]{:S(2)}) %copy-start.1) | copy-done | bytes 1048600
  1.9 0.0 copy-start.3
  1.9 0.9 copy-done.3
  2.8 0.0 copy-start.6
  2.8 0.7 copy-done.6
  3.5 0.0 copy-start.8
  3.5 0.7 copy-done.8
  4.2 32.9 %shard_map.93 = (bf16[4096,128]{1,0:T(8,128)(2,1)S(1)}, bf16[1024,128]{1,0:T(8,128)(2,1)S(1)}) custom-call(bf16[128,4096]{1,0:T(8,128)(2,1)S(1)} %bitcast.9, s32[1,32]{1,0:T(1,128)S(1)} %copy-done.6, s32[1,32]{1,0:T(1,128)S(1)} %copy-done.8, bf16[32,4096]{1,0:T(8,128)(2,1)S(1)} %bitcast.11), custom_call_target="tpu_custom_call" | custom-call | tf_op jit(solution)/shard_map/pallas_call | solution.py:473
  37.0 0.0 copy-start.2
  37.0 1.0 copy-done.2
  38.0 0.0 copy-start.4
  38.0 0.7 copy-done.4
  38.7 22.3 %shard_map.94 = (bf16[1024,128]{1,0:T(8,128)(2,1)}, f32[4096,128]{1,0:T(8,128)}, f32[2,128]{1,0:T(2,128)}) custom-call(bf16[4096,128]{1,0:T(8,128)(2,1)} %copy-done.2, bf16[1024,128]{1,0:T(8,128)(2,1)} %copy-done.4, f32[32,128]{1,0:T(8,128)} %bitcast.14, f32[32,128]{1,0:T(8,128)} %bitcast.15), custom_call_target="tpu_custom_call" | custom-call | tf_op jit(solution)/shard_map/pallas_call | solution.py:489
  61.0 0.0 copy-done.9
  61.0 0.0 copy-done.7
  61.0 0.0 copy-start
  61.0 1.6 %copy-done = f32[4096,128]{1,0:T(8,128)S(1)} copy-done((f32[4096,128]{1,0:T(8,128)S(1)}, f32[4096,128]{1,0:T(8,128)}, u32[]{:S(2)}) %copy-start) | copy-done | bytes 2097176
  62.6 0.0 copy-start.5
  62.6 0.9 copy-done.5
  63.5 0.0 copy-start.10
  63.6 0.7 copy-done.10
  64.2 31.2 %shard_map.95 = (bf16[32,4096]{1,0:T(8,128)(2,1)S(1)}, f32[128,4096]{1,0:T(8,128)S(1)}, f32[32,128]{1,0:T(8,128)S(1)}, f32[32,128]{1,0:T(8,128)S(1)}) custom-call(s32[1,32]{1,0:T(1,128)S(1)} %copy-done.7, s32[1,32]{1,0:T(1,128)S(1)} %copy-done.9, bf16[1024,128]{1,0:T(8,128)(2,1)S(1)} %copy-done.5, f32[4096,128]{1,0:T(8,128)S(1)} %copy-done, ...), custom_call_target="tpu_custom_call" | custom-call | tf_op jit(solution)/shard_map/pallas_call | solution.py:497
  95.4 0.7 copy.14
  96.1 1.3 %copy.15 = f32[1,128,4096]{2,1,0:T(8,128)} copy(f32[1,128,4096]{2,1,0:T(8,128)S(1)} %bitcast.8) | data formatting | bytes 4194304
  97.4 0.6 copy.16
  98.0 0.6 copy.17
Async XLA Ops:
  0.6 60.4 %copy-start.9 = (s32[1,32]{1,0:T(1,128)S(1)}, s32[1,32]{1,0:T(1,128)}, u32[]{:S(2)}) copy-start(s32[1,32]{1,0:T(1,128)} %lengths.3) | copy-start | bytes 388
  0.6 60.4 %copy-start.7 = (s32[1,32]{1,0:T(1,128)S(1)}, s32[1,32]{1,0:T(1,128)}, u32[]{:S(2)}) copy-start(s32[1,32]{1,0:T(1,128)} %starts.3) | copy-start | bytes 388
  0.7 1.2 %copy-start.1 = (bf16[1,128,4096]{2,1,0:T(8,128)(2,1)S(1)}, bf16[1,128,4096]{2,1,0:T(8,128)(2,1)}, u32[]{:S(2)}) copy-start(bf16[1,128,4096]{2,1,0:T(8,128)(2,1)} %param.6) | copy-start | bytes 3145732
  1.9 0.9 copy-start.3
  2.8 0.7 copy-start.6
  3.5 0.7 copy-start.8
  37.0 1.0 copy-start.2
  38.0 0.7 copy-start.4
  61.0 1.6 %copy-start = (f32[4096,128]{1,0:T(8,128)S(1)}, f32[4096,128]{1,0:T(8,128)}, u32[]{:S(2)}) copy-start(f32[4096,128]{1,0:T(8,128)} %get-tuple-element.16.side) | copy-start | bytes 6291460
  62.6 0.9 copy-start.5
  63.5 0.7 copy-start.10

commit v2 on v0

v2 whole, which is shorter than its diff:
```python
import functools
import math

import jax
import jax.numpy as jnp
from jax import lax
from jax.experimental import pallas as pl
from jax.experimental.pallas import tpu as pltpu
from jax.sharding import PartitionSpec as P

f32 = jnp.float32
bf16 = jnp.bfloat16
HEAD_DIM = 128
HEADS = 32
PIECE = 32
BLOCK = 512
EPS = 1e-6
NT = (((1,), (1,)), ((), ()))
TN = (((0,), (0,)), ((), ()))


def place():
    seq = lax.axis_index("seq")
    core = lax.axis_index("dp")
    y = seq // 32
    return seq, core, y, (seq // 8) % 4, seq % 8


def at(seq, core):
    return {"seq": seq, "dp": core}


def low_block(y, core):
    return core + 2 * (((y + 1) // 2) % 2)


def owner(y, x, doc):
    block = 2 * y + x // 2
    high = block // 4
    low = block + high * (7 - 2 * block)
    half = low // 2
    return (doc * (3 - half) + (1 - doc) * half), low % 2, high


def source(y, core, i):
    low = low_block(y, core)
    high = i // 16
    block = low + high * (7 - 2 * low)
    return block * 16 + i % 16, y // 2, i * PIECE


def head_at(x, z, i):
    return ((x + i // 8) % 4) * 8 + (z + i % 8) % 8


MESH = pl.DeviceIdType.MESH


def signal(sem, seq, core):
    pl.semaphore_signal(sem, inc=1, device_id=at(seq, core), device_id_type=MESH)


def remote(src, dst, send, recv, seq, core):
    return pltpu.make_async_remote_copy(
        src_ref=src, dst_ref=dst, send_sem=send, recv_sem=recv,
        device_id=at(seq, core), device_id_type=MESH,
    )


def column(row, count):
    r = lax.broadcasted_iota(jnp.int32, (count, count), 0)
    c = lax.broadcasted_iota(jnp.int32, (count, count), 1)
    return jnp.sum(jnp.where(r == c, jnp.broadcast_to(row, (count, count)), 0), 1, keepdims=True)


SCALE = HEAD_DIM ** -0.5
C2 = SCALE * math.log2(math.e)
STEPS = 9
GROUP = BLOCK // HEAD_DIM


def chunk(j):
    return pl.ds(pl.multiple_of(j * BLOCK, BLOCK), BLOCK)


def lanes(x, op):
    parts = [x[:, g * HEAD_DIM:(g + 1) * HEAD_DIM] for g in range(x.shape[1] // HEAD_DIM)]
    return functools.reduce(op, parts)


def step_at(low, t):
    if isinstance(t, int):
        return {0: (0, low), 7: (1, low), 8: (1, 7 - low)}[t]
    high = (t - low + 7) // 8
    place = t - low - 1
    return high, high * (place + (place - low + 8) // 8) + (1 - high) * (low - t)


def over_steps(body, waits=None):
    body((0, 8, 7))
    if waits is not None:
        waits()

    def three(i, _):
        body(tuple(1 + 3 * i + u for u in range(3)))
        return 0

    lax.fori_loop(0, 2, three, 0)


def tiled(x):
    return jnp.concatenate([x] * GROUP, 1)


def forward(low, kfull, keyed, query, s_ref, w_ref, stat, mixed, waits=None):
    stat[...] = jnp.full(stat.shape, -1e30, f32)

    def cols(t):
        return pl.ds(pl.multiple_of(t * BLOCK, BLOCK), BLOCK)

    def scores(steps):
        for t in steps:
            high, j = step_at(low, t)
            s = lax.dot_general(query[chunk(high), :], keyed[chunk(j), :], NT, preferred_element_type=f32)
            if isinstance(t, int) and t != 7:
                r = lax.broadcasted_iota(jnp.int32, s.shape, 0)
                c = lax.broadcasted_iota(jnp.int32, s.shape, 1)
                s = jnp.where(c <= r, s, -1e30)
            s_ref[:, cols(t)] = s
            stat[chunk(high), :] = jnp.maximum(stat[chunk(high), :], lanes(s, jnp.maximum))

    over_steps(scores, waits)
    stat[...] = jnp.broadcast_to(jnp.max(stat[...], -1, keepdims=True), stat.shape)
    mixed[...] = jnp.zeros(mixed.shape, f32)

    def expo(steps):
        for t in steps:
            high, j = step_at(low, t)
            e = jnp.exp2((s_ref[:, cols(t)] - tiled(stat[chunk(high), :])) * C2)
            s_ref[:, cols(t)] = e
            mixed[chunk(high), :] += lanes(e, jnp.add)

    over_steps(expo)
    stat[...] = jnp.broadcast_to(1.0 / jnp.sum(mixed[...], -1, keepdims=True), stat.shape)
    mixed[...] = jnp.zeros(mixed.shape, f32)

    def mix(steps):
        for t in steps:
            high, j = step_at(low, t)
            w = (s_ref[:, cols(t)] * tiled(stat[chunk(high), :])).astype(bf16)
            w_ref[:, cols(t)] = w
            mixed[chunk(high), :] += jnp.dot(w, kfull[chunk(j), :], preferred_element_type=f32)

    over_steps(mix)


def normed(mixed, out):
    m = mixed[...]
    rs = 1.0 / jnp.sqrt(jnp.mean(m * m, -1, keepdims=True) + EPS)
    out[...] = (m * rs).astype(bf16)
    return rs


def backward(low, kfull, keyed, query, dmb, s_ref, w_ref, d_ref, stat, delta, dk, dv, dq):
    def cols(t):
        return pl.ds(pl.multiple_of(t * BLOCK, BLOCK), BLOCK)

    delta[...] = jnp.zeros(delta.shape, f32)

    def dprobs(steps):
        for t in steps:
            high, j = step_at(low, t)
            dp = lax.dot_general(dmb[chunk(high), :], kfull[chunk(j), :], NT, preferred_element_type=f32)
            d_ref[:, cols(t)] = dp
            dv[chunk(j), :] += lax.dot_general(w_ref[:, cols(t)], dmb[chunk(high), :], TN, preferred_element_type=f32)
            delta[chunk(high), :] += lanes(dp * s_ref[:, cols(t)], jnp.add)

    over_steps(dprobs)
    delta[...] = jnp.broadcast_to(jnp.sum(delta[...], -1, keepdims=True), delta.shape) * stat[...]
    stat[...] = stat[...] * SCALE
    dq[...] = jnp.zeros(dq.shape, f32)

    def back(steps):
        for t in steps:
            high, j = step_at(low, t)
            ds = ((s_ref[:, cols(t)] * tiled(stat[chunk(high), :]))
                  * (d_ref[:, cols(t)] - tiled(delta[chunk(high), :]))).astype(bf16)
            dk[chunk(j), :] += lax.dot_general(ds, query[chunk(high), :], TN, preferred_element_type=f32)
            dq[chunk(high), :] += jnp.dot(ds, keyed[chunk(j), :], preferred_element_type=f32)

    over_steps(back)


def whole(states, starts, lengths, qgain_all, kgain_all, cot_rows,
          patch_out, dpool, spill_back, plane,
          bytes_in, cot, pooled, sums, spill, spill_in, back, kfull, cot_h, out_h,
          keyed, query, s_ref, w_ref, d_ref, dk, dv, dq, stat, delta, mixed, dmb,
          from_sib, to_far, from_far, mine_b, column_in,
          s_load, s_spill, r_spill, s_pool, r_pool, s_cot, r_cot, s_key, r_key,
          s_out, r_out, s_sib, r_sib, s_far, r_far, s_dp, r_dp, s_col, r_col, s_pla, r_pla,
          s_back, r_back):
    seq, core, y, x, z = place()
    oy, ocore, ohigh = owner(y, x, core)
    mine = (oy == y) & (ocore == core)
    low = low_block(y, core)
    sib = low + 1 - 2 * (low % 2)
    far = low + 2 - 4 * (low // 2)
    farsib = sib + 2 - 4 * (sib // 2)
    partner = seq + 32 - 64 * (y % 2)
    before = (seq + 127) % 128
    after = (seq + 1) % 128
    head = x * 8 + z

    load_bytes = pltpu.make_async_copy(states, bytes_in, s_load.at[0])
    load_cot = pltpu.make_async_copy(cot_rows, cot, s_load.at[1])
    load_bytes.start()
    load_cot.start()

    barrier = pltpu.get_barrier_semaphore()

    def greet(i, _):
        s, d, _row = source(y, core, (i + head) % 32)

        @pl.when((s != seq) | (d != core))
        def _():
            signal(barrier, s, d)

        return 0

    lax.fori_loop(0, 32, greet, 0)

    def greet_column(i, _):
        c = (y * 2 + core + i) % 8
        signal(barrier, (c // 2) * 32 + head, c % 2)
        return 0

    lax.fori_loop(1, 8, greet_column, 0)
    signal(barrier, after, core)

    base = seq * 128
    start = column(starts[...], PIECE) - base
    length = column(lengths[...], PIECE)
    at_byte = lax.broadcasted_iota(jnp.int32, (PIECE, 128), 1)
    member = ((at_byte >= start) & (at_byte < start + length)).astype(f32).astype(bf16)
    first = starts[:, 0:1] - base
    lead = (lax.broadcasted_iota(jnp.int32, (16, 128), 1) < first).astype(f32).astype(bf16)
    inverse = 1.0 / length.astype(f32)
    load_bytes.wait()
    spill[...] = jnp.dot(lead, bytes_in[...], preferred_element_type=f32)[0:1, :]
    sums[...] = jnp.dot(member, bytes_in[...], preferred_element_type=f32) * inverse

    @pl.when(mine)
    def _():
        pl.semaphore_wait(barrier, 31 + 7 + 1)

    @pl.when(jnp.logical_not(mine))
    def _():
        pl.semaphore_wait(barrier, 32 + 7 + 1)

    spilling = remote(spill, spill_in, s_spill, r_spill, before, core)
    spilling.start()

    def scatter_rows(src, dst, row, first_row, count, send, recv):
        def step(i, _):
            h = head_at(x, z, i)
            part = src.at[pl.ds(first_row, count), pl.ds(pl.multiple_of(h * HEAD_DIM, HEAD_DIM), HEAD_DIM)]
            there = dst.at[pl.ds(pl.multiple_of(row + first_row, 16), count), :]
            target = oy * 32 + h
            local = (target == seq) & (ocore == core)

            @pl.when(local)
            def _():
                pltpu.make_async_copy(part, there, recv).start()

            @pl.when(jnp.logical_not(local))
            def _():
                remote(part, there, send, recv, target, ocore).start()

            return 0

        lax.fori_loop(0, 32, step, 0)

    pooled[0:16, :] = sums[0:16, :].astype(bf16)
    scatter_rows(pooled, kfull, seq * PIECE, 0, 16, s_pool, r_pool)
    spilling.wait_recv()
    last = (lax.broadcasted_iota(jnp.int32, (16, 1), 0) == 15) & (seq < 127)
    pooled[16:32, :] = (sums[16:32, :] + jnp.where(last, spill_in[...] * inverse[16:32, :], 0.0)).astype(bf16)
    scatter_rows(pooled, kfull, seq * PIECE, 16, 16, s_pool, r_pool)
    load_cot.wait()
    scatter_rows(cot, cot_h, ohigh * BLOCK + (seq % 16) * PIECE, 0, PIECE, s_cot, r_cot)

    qgain = qgain_all[pl.ds(head, 1), :]
    kgain = kgain_all[pl.ds(head, 1), :]

    def clear(j, _):
        dk[chunk(j), :] = jnp.zeros((BLOCK, HEAD_DIM), f32)
        dv[chunk(j), :] = jnp.zeros((BLOCK, HEAD_DIM), f32)
        return 0

    lax.fori_loop(0, 8, clear, 0)

    pltpu.make_async_copy(kfull.at[pl.ds(0, 1024), :], kfull.at[pl.ds(0, 1024), :], r_pool).wait()
    across, beside = [], []
    for i, block in enumerate((low, 7 - low)):
        there = kfull.at[chunk(block), :]
        across.append(remote(there, there, s_key.at[i], r_key.at[i], partner, core))
        beside.append(remote(there, there, s_key.at[2 + i], r_key.at[2 + i], seq, 1 - core))
        across[i].start()
        beside[i].start()

    def prepare(block):
        keyed[chunk(block), :] = (kfull[chunk(block), :].astype(f32) * kgain).astype(bf16)

    for i, block in enumerate((low, 7 - low)):
        query[chunk(i), :] = (kfull[chunk(block), :].astype(f32) * qgain).astype(bf16)
        prepare(block)

    relays = []

    def other_keys():
        for i, block in enumerate((sib, 7 - sib)):
            beside[i].wait_recv()
            prepare(block)
        for i, block in enumerate((far, 7 - far)):
            across[i].wait_recv()
            there = kfull.at[chunk(block), :]
            relays.append(remote(there, there, s_key.at[4 + i], r_key.at[4 + i], seq, 1 - core))
            relays[i].start()
            prepare(block)
        for i, block in enumerate((farsib, 7 - farsib)):
            relays[i].wait_recv()
            prepare(block)

    forward(low, kfull, keyed, query, s_ref, w_ref, stat, mixed, other_keys)
    rs = normed(mixed, out_h)

    head_columns = pl.ds(pl.multiple_of(head * HEAD_DIM, HEAD_DIM), HEAD_DIM)

    def scatter_back(src, dst, send, recv):
        def step(i, _):
            s, d, row = source(y, core, (i + head) % 32)
            part = src.at[pl.ds(pl.multiple_of(row, PIECE), PIECE), :]
            there = dst.at[:, head_columns]
            local = (s == seq) & (d == core)

            @pl.when(local)
            def _():
                pltpu.make_async_copy(part, there, recv).start()

            @pl.when(jnp.logical_not(local))
            def _():
                remote(part, there, send, recv, s, d).start()

            return 0

        lax.fori_loop(0, 32, step, 0)

    scatter_back(out_h, patch_out, s_out, r_out)
    pltpu.make_async_copy(cot_h, cot_h, r_cot).wait()
    g = cot_h[...].astype(f32)
    m = mixed[...]
    dmb[...] = (g * rs - m * (jnp.sum(g * m, -1, keepdims=True) * (rs * rs * rs) * (1.0 / HEAD_DIM))).astype(bf16)
    backward(low, kfull, keyed, query, dmb, s_ref, w_ref, d_ref, stat, delta, dk, dv, dq)

    gk = jnp.zeros((1, HEAD_DIM), f32)
    to_sib = []
    for i, block in enumerate((farsib, 7 - farsib, sib, 7 - sib, far, 7 - far, low, 7 - low)):
        d = dk[chunk(block), :]
        dv[chunk(block), :] += d * kgain
        gk = gk + jnp.sum(d * kfull[chunk(block), :].astype(f32), 0, keepdims=True)
        if i < 4:
            to_sib.append(remote(dv.at[chunk(block), :], from_sib.at[i], s_sib.at[i], r_sib.at[i], seq, 1 - core))
            to_sib[i].start()
    gq = jnp.zeros((1, HEAD_DIM), f32)
    for i, block in enumerate((low, 7 - low)):
        gq = gq + jnp.sum(dq[chunk(i), :] * kfull[chunk(block), :].astype(f32), 0, keepdims=True)
    place_in_column = pl.ds(y * 2 + core, 1)
    column_in[place_in_column] = jnp.concatenate([gq, gk], 0)[None]

    def send_column(i, _):
        c = (y * 2 + core + i) % 8
        slot = column_in.at[place_in_column]
        remote(slot, slot, s_col, r_col, (c // 2) * 32 + head, c % 2).start()
        return 0

    lax.fori_loop(1, 8, send_column, 0)

    to_partner = []
    for i, block in enumerate((far, 7 - far)):
        to_sib[i].wait_recv()
        to_far[i] = (dv[chunk(block), :] + from_sib[i]).astype(bf16)
        to_partner.append(remote(to_far.at[i], from_far.at[i], s_far.at[i], r_far.at[i], partner, core))
        to_partner[i].start()
    for i, block in enumerate((low, 7 - low)):
        to_sib[2 + i].wait_recv()
        mixed[chunk(i), :] = dv[chunk(block), :] + from_sib[2 + i] + dq[chunk(i), :] * qgain

    pltpu.make_async_copy(column_in.at[0:7], column_in.at[0:7], r_col).wait()
    total = column_in[0]
    for i in range(1, 8):
        total = total + column_in[i]
    pltpu.make_async_copy(column_in.at[0:7], column_in.at[0:7], s_col).wait()
    column_in[place_in_column] = total[None]

    def send_plane(i, _):
        s, d, _row = source(y, core, (i + head) % 32)
        part = column_in.at[place_in_column]
        there = plane.at[pl.ds(head, 1)]
        local = (s == seq) & (d == core)

        @pl.when(local)
        def _():
            pltpu.make_async_copy(part, there, r_pla).start()

        @pl.when(jnp.logical_not(local))
        def _():
            remote(part, there, s_pla, r_pla, s, d).start()

        return 0

    lax.fori_loop(0, 32, send_plane, 0)

    for i in range(2):
        to_partner[i].wait_recv()
        mine_b[chunk(i), :] = (mixed[chunk(i), :] + from_far[i].astype(f32)).astype(bf16)
    scatter_back(mine_b, dpool, s_dp, r_dp)

    pltpu.make_async_copy(dpool, dpool, r_dp).wait()
    back[...] = dpool[16:32, :].astype(f32)[15:16, :] * inverse[PIECE - 1:PIECE, :]
    returning = remote(back, spill_back, s_back, r_back, after, core)
    returning.start()
    returning.wait_recv()

    pltpu.make_async_copy(patch_out, patch_out, r_out).wait()
    pltpu.make_async_copy(plane, plane, r_pla).wait()
    returning.wait_send()
    spilling.wait_send()
    for copy in across + beside + relays + to_sib + to_partner:
        copy.wait_send()

    @pl.when(mine)
    def _():
        for src, sem in ((pooled, s_pool), (cot, s_cot)):
            part = src.at[:, pl.ds(0, 31 * HEAD_DIM)]
            pltpu.make_async_copy(part, part, sem).wait()
        for src, sem in ((out_h, s_out), (mine_b, s_dp)):
            part = src.at[0:31 * PIECE]
            pltpu.make_async_copy(part, part, sem).wait()
        pltpu.make_async_copy(plane.at[0:31], plane.at[0:31], s_pla).wait()

    @pl.when(jnp.logical_not(mine))
    def _():
        for src, sem in ((pooled, s_pool), (cot, s_cot), (out_h, s_out), (mine_b, s_dp), (plane, s_pla)):
            pltpu.make_async_copy(src, src, sem).wait()


def finish(starts, lengths, dpool, spill_back, out_in, plane, grad, patch_out, gq, gk):
    base = lax.axis_index("seq") * 128
    start = starts[...] - base
    length = lengths[...]
    at_byte = lax.broadcasted_iota(jnp.int32, (128, PIECE), 0)
    inside = (at_byte >= start) & (at_byte < start + length)
    member = inside.astype(f32).astype(bf16)
    by_byte = jnp.sum(jnp.where(inside, 1.0 / length.astype(f32), 0.0), 1, keepdims=True)
    lead = lax.broadcasted_iota(jnp.int32, (8, 1), 0) < start[:, 0:1]
    grad[...] = jnp.dot(member, dpool[...], preferred_element_type=f32) * by_byte
    grad[0:8, :] = jnp.where(lead, spill_back[...], grad[0:8, :])
    patch_out[...] = out_in[...]

    @pl.when(pl.program_id(0) == 0)
    def _():
        for i in range(HEADS):
            gq[i:i + 1, :] = plane[i, 0:1, :]
            gk[i:i + 1, :] = plane[i, 1:2, :]


VMEM = pl.BlockSpec(memory_space=pltpu.VMEM)
ANY = pl.BlockSpec(memory_space=pl.ANY)
DMA = pltpu.SemaphoreType.DMA
PARTS = 4


def shape(dims, dtype):
    return jax.ShapeDtypeStruct(dims, dtype)


def on_device(byte_states, patch_starts, patch_lengths, query_gain, key_gain, out_cotangent):
    states = byte_states[0]
    cot = out_cotangent[0]
    width = states.shape[1]
    own = 2 * BLOCK
    keys = 8 * BLOCK
    V = pltpu.VMEM
    out_rows, dpool, spill_back, plane = pl.pallas_call(
        whole,
        out_shape=(shape((PIECE, width), bf16), shape((PIECE, width), bf16), shape((1, width), f32),
                   shape((HEADS, 2, HEAD_DIM), f32)),
        in_specs=[ANY, VMEM, VMEM, VMEM, VMEM, ANY],
        out_specs=(VMEM,) * 4,
        scratch_shapes=[
            V((128, width), bf16), V((PIECE, width), bf16), V((PIECE, width), bf16), V((PIECE, width), f32),
            V((1, width), f32), V((1, width), f32), V((1, width), f32),
            V((keys, HEAD_DIM), bf16), V((own, HEAD_DIM), bf16), V((own, HEAD_DIM), bf16),
            V((keys, HEAD_DIM), bf16), V((own, HEAD_DIM), bf16),
            V((BLOCK, STEPS * BLOCK), f32), V((BLOCK, STEPS * BLOCK), bf16), V((BLOCK, STEPS * BLOCK), f32),
            V((keys, HEAD_DIM), f32), V((keys, HEAD_DIM), f32),
            V((own, HEAD_DIM), f32), V((own, HEAD_DIM), f32), V((own, HEAD_DIM), f32), V((own, HEAD_DIM), f32),
            V((own, HEAD_DIM), bf16),
            V((4, BLOCK, HEAD_DIM), f32), V((2, BLOCK, HEAD_DIM), bf16), V((2, BLOCK, HEAD_DIM), bf16),
            V((own, HEAD_DIM), bf16), V((8, 2, HEAD_DIM), f32),
            DMA((2,)), DMA, DMA, DMA, DMA, DMA, DMA, DMA((6,)), DMA((6,)),
            DMA, DMA, DMA((4,)), DMA((4,)), DMA((2,)), DMA((2,)), DMA, DMA, DMA, DMA, DMA, DMA,
            DMA, DMA,
        ],
        compiler_params=pltpu.CompilerParams(
            collective_id=0, has_side_effects=True, vmem_limit_bytes=56 << 20
        ),
    )(states, patch_starts, patch_lengths, query_gain.reshape(HEADS, HEAD_DIM), key_gain.reshape(HEADS, HEAD_DIM), cot)
    part = width // PARTS

    def columns(rows):
        return pl.BlockSpec((rows, part), lambda i: (0, i))

    grad, patch_out, gq, gk = pl.pallas_call(
        finish,
        grid=(PARTS,),
        out_shape=(shape((128, width), f32), shape((PIECE, width), bf16),
                   shape((HEADS, HEAD_DIM), f32), shape((HEADS, HEAD_DIM), f32)),
        in_specs=[VMEM, VMEM, columns(PIECE), columns(1), columns(PIECE), VMEM],
        out_specs=(columns(128), columns(PIECE), VMEM, VMEM),
        compiler_params=pltpu.CompilerParams(vmem_limit_bytes=16 << 20),
    )(patch_starts, patch_lengths, dpool, spill_back, out_rows, plane)
    return patch_out[None], grad[None], gq.reshape(width), gk.reshape(width)


def solution(mesh):
    rows = P("dp", "seq", None)
    flat = P("dp", "seq")
    return jax.shard_map(
        on_device,
        mesh=mesh,
        in_specs=(rows, flat, flat, P(), P(), rows),
        out_specs=(rows, rows, P(), P()),
        check_vma=False,
    )
```

time: 272 us -> 79.2 us (0.29)
  blocking collectives: 80.1 us -> 0 us
  Pallas kernels: 0 us -> 73.5 us
  starting transfers between devices: 52.6 us -> 0 us
  waiting for transfers between devices: 49.8 us -> 0 us
  matrix products: 34.2 us -> 0 us
  other arithmetic: 31 us -> 0 us
  local copies, waits for them, and re-layouts: 21.6 us -> 4.68 us
    psum x1 -> x0, blocking collectives: 80.1 us -> none  [on_device(): grad_qgain, grad_kgain = lax.psum((qgain_vec, kgain_vec), ('seq', 'dp'))]
    pallas_call x0 -> x2, Pallas kernels: none -> 73.5 us  [the longest x1 71.1 us: on_device(): pl.pallas_call(whole, out_shape=(shape((PIECE, width), bf16), shape((PIEC...]
    all_to_all x4 -> x0, starting transfers between devices: 44.4 us -> none  [the longest x1 17.9 us: on_device(): lax.all_to_all(to_heads_layout(pooled, heads, width), 'seq', split_axis=0...]
    dot_general x14 -> x0, matrix products: 34.2 us -> none  [the longest x2 12.3 us: attend_block(): lax.dot_general(weights, dmixed_b, (((0,), (0,)), ((), ())), preferred_el...]
    ppermute x8 -> x0, waiting for transfers between devices: 28 us -> none  [the longest x6 24.6 us: from_behind(): return lax.ppermute(value, axis, pairs)]
    all_to_all x4 -> x0, waiting for transfers between devices: 21.8 us -> none  [the longest x1 12.6 us: on_device(): lax.all_to_all(to_heads_layout(pooled, heads, width), 'seq', split_axis=0...]
    convert_element_type x7 -> x0, other arithmetic: 13.8 us -> none  [the longest x2 11.1 us: attend_block(): dscaled = (dscores * scale).astype(jnp.bfloat16)]
    while x48 -> x0, local copies, waits for them, and re-layouts: 10.6 us -> none
  transfers between devices with their start and end apart: 12 -> 0, of which waited for: 9 -> 0; matrix products, arithmetic and copies ran while one was open for 5% -> 0% of each run, Pallas kernels for 0% -> 0%
where the time goes in v2:
time: 79.2 us; the launch traced here: 78.8 us
  Pallas kernels  73.5 us (93%)
  local copies, waits for them, and re-layouts  4.68 us (6%)
    pallas_call x1, Pallas kernels, on_device(): pl.pallas_call(whole, out_shape=(shape((PIECE, width), bf16), shape((PIEC...  71.1 us
    unnamed x12, local copies, waits for them, and re-layouts  4.68 us
    pallas_call x1, Pallas kernels, on_device(): pl.pallas_call(finish, grid=(PARTS,), out_shape=(shape((128, width), f32)...  2.37 us

profile of v2, /device:TPU:1, one launch (start us, length us, event | category | flops | bytes accessed | tf_op | source)
XLA Modules:
  0.0 78.8 jit_solution(11086966790892204101)
XLA Ops:
  0.6 71.1 %shard_map.93 = (bf16[32,4096]{1,0:T(8,128)(2,1)}, bf16[32,4096]{1,0:T(8,128)(2,1)}, f32[1,4096]{1,0:T(1,128)}, f32[32,2,128]{2,1,0:T(2,128)}) custom-call(bf16[128,4096]{1,0:T(8,128)(2,1)} %bitcast.8, s32[1,32]{1,0:T(1,128)} %starts.3, s32[1,32]{1,0:T(1,128)} %lengths.3, f32[32,128]{1,0:T(8,128)} %bitcast.10, f32[32,128]{1,0:T(8,128)} %bitcast.11, ...), custom_call_target="tpu_custom_call" | custom-call | tf_op jit(solution)/shard_map/pallas_call | solution.py:494
  71.8 0.0 copy-start
  71.8 0.9 %copy-done = bf16[32,4096]{1,0:T(8,128)(2,1)S(1)} copy-done((bf16[32,4096]{1,0:T(8,128)(2,1)S(1)}, bf16[32,4096]{1,0:T(8,128)(2,1)}, u32[]{:S(2)}) %copy-start) | copy-done | bytes 262168
  72.7 0.0 copy-start.1
  72.7 0.9 %copy-done.1 = bf16[32,4096]{1,0:T(8,128)(2,1)S(1)} copy-done((bf16[32,4096]{1,0:T(8,128)(2,1)S(1)}, bf16[32,4096]{1,0:T(8,128)(2,1)}, u32[]{:S(2)}) %copy-start.1) | copy-done | bytes 262168
  73.7 0.0 copy-start.2
  73.7 0.8 copy-done.2
  74.4 0.0 copy-start.3
  74.4 0.7 copy-done.3
  75.2 0.0 copy-start.4
  75.2 0.7 copy-done.4
  75.8 0.0 copy-start.5
  75.8 0.7 copy-done.5
  76.5 2.4 %shard_map.94 = (f32[128,4096]{1,0:T(8,128)}, bf16[32,4096]{1,0:T(8,128)(2,1)}, f32[32,128]{1,0:T(8,128)}, f32[32,128]{1,0:T(8,128)}) custom-call(s32[1,32]{1,0:T(1,128)S(1)} %copy-done.4, s32[1,32]{1,0:T(1,128)S(1)} %copy-done.5, bf16[32,4096]{1,0:T(8,128)(2,1)S(1)} %copy-done.1, f32[1,4096]{1,0:T(1,128)S(1)} %copy-done.3, bf16[32,4096]{1,0:T(8,128)(2,1)S(1)} %copy-done, ...), custom_call_target="tpu_custom_call" | custom-call | tf_op jit(solution)/shard_map/pallas_call | solution.py:524
Async XLA Ops:
  71.8 1.0 %copy-start = (bf16[32,4096]{1,0:T(8,128)(2,1)S(1)}, bf16[32,4096]{1,0:T(8,128)(2,1)}, u32[]{:S(2)}) copy-start(bf16[32,4096]{1,0:T(8,128)(2,1)} %get-tuple-element.14.out_in) | copy-start | bytes 786436
  72.7 0.9 %copy-start.1 = (bf16[32,4096]{1,0:T(8,128)(2,1)S(1)}, bf16[32,4096]{1,0:T(8,128)(2,1)}, u32[]{:S(2)}) copy-start(bf16[32,4096]{1,0:T(8,128)(2,1)} %get-tuple-element.12.dpool) | copy-start | bytes 786436
  73.7 0.8 copy-start.2
  74.4 0.7 copy-start.3
  75.2 0.7 copy-start.4
  75.8 0.7 copy-start.5

commit v3 on v2

v3 whole, which is shorter than its diff:
```python
import functools
import math

import jax
import jax.numpy as jnp
from jax import lax
from jax.experimental import pallas as pl
from jax.experimental.pallas import tpu as pltpu
from jax.sharding import PartitionSpec as P

f32 = jnp.float32
bf16 = jnp.bfloat16
HEAD_DIM = 128
HEADS = 32
PIECE = 32
BLOCK = 512
EPS = 1e-6
NT = (((1,), (1,)), ((), ()))
TN = (((0,), (0,)), ((), ()))


def place():
    seq = lax.axis_index("seq")
    core = lax.axis_index("dp")
    y = seq // 32
    return seq, core, y, (seq // 8) % 4, seq % 8


def at(seq, core):
    return {"seq": seq, "dp": core}


def low_block(y, core):
    return core + 2 * (((y + 1) // 2) % 2)


def owner(y, x, doc):
    block = 2 * y + x // 2
    high = block // 4
    low = block + high * (7 - 2 * block)
    half = low // 2
    return (doc * (3 - half) + (1 - doc) * half), low % 2, high


def source(y, core, i):
    low = low_block(y, core)
    high = i // 16
    block = low + high * (7 - 2 * low)
    return block * 16 + i % 16, y // 2, i * PIECE


def head_at(x, z, i):
    return ((x + i // 8) % 4) * 8 + (z + i % 8) % 8


MESH = pl.DeviceIdType.MESH


def signal(sem, seq, core):
    pl.semaphore_signal(sem, inc=1, device_id=at(seq, core), device_id_type=MESH)


def remote(src, dst, send, recv, seq, core):
    return pltpu.make_async_remote_copy(
        src_ref=src, dst_ref=dst, send_sem=send, recv_sem=recv,
        device_id=at(seq, core), device_id_type=MESH,
    )


def column(row, count):
    r = lax.broadcasted_iota(jnp.int32, (count, count), 0)
    c = lax.broadcasted_iota(jnp.int32, (count, count), 1)
    return jnp.sum(jnp.where(r == c, jnp.broadcast_to(row, (count, count)), 0), 1, keepdims=True)


SCALE = HEAD_DIM ** -0.5
C2 = SCALE * math.log2(math.e)
STEPS = 9
GROUP = BLOCK // HEAD_DIM


def chunk(j):
    return pl.ds(pl.multiple_of(j * BLOCK, BLOCK), BLOCK)


def lanes(x, op):
    parts = [x[:, g * HEAD_DIM:(g + 1) * HEAD_DIM] for g in range(x.shape[1] // HEAD_DIM)]
    return functools.reduce(op, parts)


def step_at(low, t):
    if isinstance(t, int) and t in (0, 7, 8):
        return {0: (0, low), 7: (1, low), 8: (1, 7 - low)}[t]
    mask = 3 - (t - 1) // 2
    second = (t - 1) % 2
    odd, far = mask % 2, mask // 2
    chunk_low = (low + odd) % 2 + 2 * ((low // 2 + far) % 2)
    mirrored = second * (far * (1 - low // 2) + (1 - far) * (1 - low % 2))
    return 1 - second + mirrored, chunk_low + mirrored * (7 - 2 * chunk_low)


def over_steps(body, between=None):
    body((0, 8, 7))
    if between is not None:
        between()

    def three(i, _):
        body(tuple(1 + 3 * i + u for u in range(3)))
        return 0

    lax.fori_loop(0, 2, three, 0)


def tiled(x):
    return jnp.concatenate([x] * GROUP, 1)


def forward(low, values, keyed, query, s_ref, w_ref, stat, mixed, between):
    stat[...] = jnp.full(stat.shape, -1e30, f32)

    def cols(t):
        return pl.ds(pl.multiple_of(t * BLOCK, BLOCK), BLOCK)

    def scores(steps):
        for t in steps:
            high, j = step_at(low, t)
            s = lax.dot_general(query[chunk(high), :], keyed[chunk(j), :], NT, preferred_element_type=f32)
            if isinstance(t, int) and t != 7:
                r = lax.broadcasted_iota(jnp.int32, s.shape, 0)
                c = lax.broadcasted_iota(jnp.int32, s.shape, 1)
                s = jnp.where(c <= r, s, -1e30)
            s_ref[:, cols(t)] = s
            stat[chunk(high), :] = jnp.maximum(stat[chunk(high), :], lanes(s, jnp.maximum))

    over_steps(scores, between)
    stat[...] = jnp.broadcast_to(jnp.max(stat[...], -1, keepdims=True), stat.shape)
    mixed[...] = jnp.zeros(mixed.shape, f32)

    def expo(steps):
        for t in steps:
            high, j = step_at(low, t)
            e = jnp.exp2((s_ref[:, cols(t)] - tiled(stat[chunk(high), :])) * C2)
            s_ref[:, cols(t)] = e
            mixed[chunk(high), :] += lanes(e, jnp.add)

    over_steps(expo)
    stat[...] = jnp.broadcast_to(1.0 / jnp.sum(mixed[...], -1, keepdims=True), stat.shape)
    mixed[...] = jnp.zeros(mixed.shape, f32)

    def mix(steps):
        for t in steps:
            high, j = step_at(low, t)
            w = (s_ref[:, cols(t)] * tiled(stat[chunk(high), :])).astype(bf16)
            w_ref[:, cols(t)] = w
            mixed[chunk(high), :] += jnp.dot(w, values(j), preferred_element_type=f32)

    over_steps(mix)


def normed(mixed, out):
    m = mixed[...]
    rs = 1.0 / jnp.sqrt(jnp.mean(m * m, -1, keepdims=True) + EPS)
    out[...] = (m * rs).astype(bf16)
    return rs


def backward(low, values, keyed, query, dmb, s_ref, w_ref, d_ref, stat, delta, dk, dv, dq, after):
    def cols(t):
        return pl.ds(pl.multiple_of(t * BLOCK, BLOCK), BLOCK)

    delta[...] = jnp.zeros(delta.shape, f32)

    def dprobs(steps):
        for t in steps:
            high, j = step_at(low, t)
            dp = lax.dot_general(dmb[chunk(high), :], values(j), NT, preferred_element_type=f32)
            d_ref[:, cols(t)] = dp
            dv[chunk(j), :] += lax.dot_general(w_ref[:, cols(t)], dmb[chunk(high), :], TN, preferred_element_type=f32)
            delta[chunk(high), :] += lanes(dp * s_ref[:, cols(t)], jnp.add)

    over_steps(dprobs)
    delta[...] = jnp.broadcast_to(jnp.sum(delta[...], -1, keepdims=True), delta.shape) * stat[...]
    stat[...] = stat[...] * SCALE
    dq[...] = jnp.zeros(dq.shape, f32)

    def back(steps):
        for t in steps:
            high, j = step_at(low, t)
            ds = ((s_ref[:, cols(t)] * tiled(stat[chunk(high), :]))
                  * (d_ref[:, cols(t)] - tiled(delta[chunk(high), :]))).astype(bf16)
            dk[chunk(j), :] += lax.dot_general(ds, query[chunk(high), :], TN, preferred_element_type=f32)
            dq[chunk(high), :] += jnp.dot(ds, keyed[chunk(j), :], preferred_element_type=f32)

    for n, steps in enumerate(((1, 2), (3, 4), (5, 6), (0, 8, 7))):
        back(steps)
        after(n)


def whole(states, starts, lengths, qgain_all, kgain_all, cot_rows,
          patch_out, dpool, spill_back, plane, inverse_before,
          bytes_in, cot, pooled, sums, spill, spill_in, inverse_out, kfull, cot_h, out_h,
          keyed, query, s_ref, w_ref, d_ref, dk, dv, dq, stat, delta, mixed, dmb,
          from_sib, to_far, from_far, mine_b, last_rows, column_in,
          s_load, s_spill, r_spill, s_pool, r_pool, s_cot, r_cot, s_key, r_key,
          s_out, r_out, s_sib, r_sib, s_far, r_far, s_dp, r_dp, s_col, r_col, s_pla, r_pla,
          s_last, r_last, s_inv, r_inv):
    seq, core, y, x, z = place()
    oy, ocore, ohigh = owner(y, x, core)
    mine = (oy == y) & (ocore == core)
    low = low_block(y, core)
    sib = low + 1 - 2 * (low % 2)
    far = low + 2 - 4 * (low // 2)
    farsib = sib + 2 - 4 * (sib // 2)
    partner = seq + 32 - 64 * (y % 2)
    before = (seq + 127) % 128
    after = (seq + 1) % 128
    head = x * 8 + z
    by, bcore, _high = owner(before // 32, (before // 8) % 4, core)
    mine_before = (by == y) & (bcore == core)
    pending = []

    def wait_all(ref, sem):
        pltpu.make_async_copy(ref, ref, sem).wait()

    def sent(ref, part, sem, own=mine):
        @pl.when(own)
        def _():
            wait_all(part, sem)

        @pl.when(jnp.logical_not(own))
        def _():
            wait_all(ref, sem)

    load_bytes = pltpu.make_async_copy(states, bytes_in, s_load.at[0])
    load_cot = pltpu.make_async_copy(cot_rows, cot, s_load.at[1])
    load_bytes.start()
    load_cot.start()

    barrier = pltpu.get_barrier_semaphore()

    def greet(i, _):
        s, d, _row = source(y, core, (i + head) % 32)

        @pl.when((s != seq) | (d != core))
        def _():
            signal(barrier, s, d)

        return 0

    lax.fori_loop(0, 32, greet, 0)

    def greet_column(i, _):
        c = (y * 2 + core + i) % 8
        signal(barrier, (c // 2) * 32 + head, c % 2)
        return 0

    lax.fori_loop(1, 8, greet_column, 0)
    signal(barrier, after, core)
    signal(barrier, before, core)

    base = seq * 128
    start = column(starts[...], PIECE) - base
    length = column(lengths[...], PIECE)
    at_byte = lax.broadcasted_iota(jnp.int32, (PIECE, 128), 1)
    member = ((at_byte >= start) & (at_byte < start + length)).astype(f32).astype(bf16)
    first = starts[:, 0:1] - base
    lead = (lax.broadcasted_iota(jnp.int32, (16, 128), 1) < first).astype(f32).astype(bf16)
    inverse = 1.0 / length.astype(f32)
    inverse_out[...] = jnp.broadcast_to(inverse[PIECE - 1:PIECE, :], (1, HEAD_DIM))
    load_bytes.wait()
    spill[...] = jnp.dot(lead, bytes_in[...], preferred_element_type=f32)[0:1, :]
    sums[...] = jnp.dot(member, bytes_in[...], preferred_element_type=f32) * inverse

    @pl.when(mine)
    def _():
        pl.semaphore_wait(barrier, 31 + 7 + 2)

    @pl.when(jnp.logical_not(mine))
    def _():
        pl.semaphore_wait(barrier, 32 + 7 + 2)

    spilling = remote(spill, spill_in, s_spill, r_spill, before, core)
    spilling.start()
    telling = remote(inverse_out, inverse_before, s_inv, r_inv, after, core)
    telling.start()
    pending.extend([spilling.wait_send, telling.wait])

    def scatter_rows(src, dst, first_row, count, send, recv):
        def step(i, _):
            h = head_at(x, z, i)
            part = src.at[pl.ds(first_row, count), pl.ds(pl.multiple_of(h * HEAD_DIM, HEAD_DIM), HEAD_DIM)]
            target = oy * 32 + h
            local = (target == seq) & (ocore == core)

            @pl.when(local)
            def _():
                pltpu.make_async_copy(part, dst, recv).start()

            @pl.when(jnp.logical_not(local))
            def _():
                remote(part, dst, send, recv, target, ocore).start()

            return 0

        lax.fori_loop(0, 32, step, 0)

    columns = pl.ds(0, 31 * HEAD_DIM)
    pooled[0:16, :] = sums[0:16, :].astype(bf16)
    scatter_rows(pooled, kfull.at[seq, pl.ds(0, 16), :], 0, 16, s_pool.at[0], r_pool.at[0])
    spilling.wait_recv()
    last = (lax.broadcasted_iota(jnp.int32, (16, 1), 0) == 15) & (seq < 127)
    pooled[16:32, :] = (sums[16:32, :] + jnp.where(last, spill_in[...] * inverse[16:32, :], 0.0)).astype(bf16)
    scatter_rows(pooled, kfull.at[seq, pl.ds(16, 16), :], 16, 16, s_pool.at[1], r_pool.at[1])
    load_cot.wait()
    crow = pl.multiple_of(ohigh * BLOCK + (seq % 16) * PIECE, PIECE)
    scatter_rows(cot, cot_h.at[pl.ds(crow, PIECE), :], 0, PIECE, s_cot, r_cot)
    for i in range(2):
        half = pooled.at[pl.ds(16 * i, 16), :]
        pending.append(functools.partial(sent, half, half.at[:, columns], s_pool.at[i]))
    pending.append(functools.partial(sent, cot, cot.at[:, columns], s_cot))

    qgain = qgain_all[pl.ds(head, 1), :]
    kgain = kgain_all[pl.ds(head, 1), :]

    def clear(j, _):
        dk[chunk(j), :] = jnp.zeros((BLOCK, HEAD_DIM), f32)
        dv[chunk(j), :] = jnp.zeros((BLOCK, HEAD_DIM), f32)
        return 0

    lax.fori_loop(0, 8, clear, 0)

    def pieces(block):
        return pl.ds(block * 16, 16)

    def values(block):
        return kfull[pieces(block)].reshape(BLOCK, HEAD_DIM)

    def prepare(block):
        keyed[chunk(block), :] = (values(block).astype(f32) * kgain).astype(bf16)

    across, beside, relays = {}, {}, {}
    for half in range(2):
        rows = pl.ds(16 * half, 16)
        wait_all(kfull.at[pl.ds(0, 32), rows, :], r_pool.at[half])
        for i, block in enumerate((low, 7 - low)):
            n = 2 * half + i
            there = kfull.at[pieces(block), rows, :]
            across[n] = remote(there, there, s_key.at[n], r_key.at[n], partner, core)
            across[n].start()
            beside[n] = remote(there, there, s_key.at[4 + n], r_key.at[4 + n], seq, 1 - core)
            beside[n].start()
            pending.extend([across[n].wait_send, beside[n].wait_send])
    for i, block in enumerate((low, 7 - low)):
        query[chunk(i), :] = (values(block).astype(f32) * qgain).astype(bf16)
        prepare(block)

    def other_keys():
        for n in range(4):
            block = (far, 7 - far)[n % 2]
            across[n].wait_recv()
            there = kfull.at[pieces(block), pl.ds(16 * (n // 2), 16), :]
            relays[n] = remote(there, there, s_key.at[8 + n], r_key.at[8 + n], seq, 1 - core)
            relays[n].start()
            pending.append(relays[n].wait_send)
            beside[n].wait_recv()
        for block in (sib, 7 - sib, far, 7 - far):
            prepare(block)
        for n in range(4):
            relays[n].wait_recv()
        for block in (farsib, 7 - farsib):
            prepare(block)

    forward(low, values, keyed, query, s_ref, w_ref, stat, mixed, other_keys)
    rs = normed(mixed, out_h)

    head_columns = pl.ds(pl.multiple_of(head * HEAD_DIM, HEAD_DIM), HEAD_DIM)

    def scatter_back(first, count, part_of, there, send, recv, shift=0):
        def step(i, _):
            n = first + (i + head) % count
            s, d, row = source(y, core, n)
            s = (s + shift) % 128
            part = part_of(n)
            local = (s == seq) & (d == core)

            @pl.when(local)
            def _():
                pltpu.make_async_copy(part, there, recv).start()

            @pl.when(jnp.logical_not(local))
            def _():
                remote(part, there, send, recv, s, d).start()

            return 0

        lax.fori_loop(0, count, step, 0)

    def rows_of(ref):
        return lambda n: ref.at[pl.ds(pl.multiple_of(n * PIECE, PIECE), PIECE), :]

    scatter_back(0, 32, rows_of(out_h), patch_out.at[:, head_columns], s_out, r_out)
    pending.append(functools.partial(sent, out_h, out_h.at[0:31 * PIECE], s_out))
    pending.append(functools.partial(wait_all, patch_out, r_out))
    wait_all(cot_h, r_cot)
    g = cot_h[...].astype(f32)
    m = mixed[...]
    dmb[...] = (g * rs - m * (jnp.sum(g * m, -1, keepdims=True) * (rs * rs * rs) * (1.0 / HEAD_DIM))).astype(bf16)

    gk = [jnp.zeros((1, HEAD_DIM), f32)]
    to_sib, to_partner = [], []

    def complete(block):
        d = dk[chunk(block), :]
        dv[chunk(block), :] += d * kgain
        gk[0] = gk[0] + jnp.sum(d * values(block).astype(f32), 0, keepdims=True)

    def give_sib(block):
        i = len(to_sib)
        to_sib.append(remote(dv.at[chunk(block), :], from_sib.at[i], s_sib.at[i], r_sib.at[i], seq, 1 - core))
        to_sib[i].start()
        pending.append(to_sib[i].wait_send)

    def after_steps(n):
        blocks = ((farsib, 7 - farsib), (far, 7 - far), (sib, 7 - sib), (low, 7 - low))[n]
        for i, block in enumerate(blocks):
            complete(block)
            if n in (0, 2):
                give_sib(block)
            if n == 1:
                to_sib[i].wait_recv()
                to_far[i] = (dv[chunk(block), :] + from_sib[i]).astype(bf16)
                to_partner.append(remote(to_far.at[i], from_far.at[i], s_far.at[i], r_far.at[i], partner, core))
                to_partner[i].start()
                pending.append(to_partner[i].wait_send)

    backward(low, values, keyed, query, dmb, s_ref, w_ref, d_ref, stat, delta, dk, dv, dq, after_steps)
    for i, block in enumerate((low, 7 - low)):
        to_sib[2 + i].wait_recv()
        to_partner[i].wait_recv()
        mixed[chunk(i), :] = (dv[chunk(block), :] + from_sib[2 + i] + dq[chunk(i), :] * qgain
                              + from_far[i].astype(f32))
        mine_b[chunk(i), :] = mixed[chunk(i), :].astype(bf16)
        scatter_back(16 * i, 16, rows_of(mine_b), dpool.at[:, head_columns], s_dp, r_dp)
    pending.append(functools.partial(sent, mine_b, mine_b.at[0:31 * PIECE], s_dp))

    for i in range(32):
        last_rows[i] = mixed[i * PIECE + PIECE - 1:(i + 1) * PIECE, :]
    scatter_back(0, 32, lambda n: last_rows.at[n], spill_back.at[:, head_columns], s_last, r_last, 1)
    pending.append(functools.partial(sent, last_rows, last_rows.at[0:31], s_last, mine_before))

    gq = jnp.zeros((1, HEAD_DIM), f32)
    for i, block in enumerate((low, 7 - low)):
        gq = gq + jnp.sum(dq[chunk(i), :] * values(block).astype(f32), 0, keepdims=True)
    place_in_column = pl.ds(y * 2 + core, 1)
    column_in[place_in_column] = jnp.concatenate([gq, gk[0]], 0)[None]

    def send_column(i, _):
        c = (y * 2 + core + i) % 8
        slot = column_in.at[place_in_column]
        remote(slot, slot, s_col, r_col, (c // 2) * 32 + head, c % 2).start()
        return 0

    lax.fori_loop(1, 8, send_column, 0)
    wait_all(column_in.at[0:7], r_col)
    total = column_in[0]
    for i in range(1, 8):
        total = total + column_in[i]
    wait_all(column_in.at[0:7], s_col)
    column_in[place_in_column] = total[None]
    scatter_back(0, 32, lambda n: column_in.at[y * 2 + core], plane.at[head], s_pla, r_pla)
    pending.append(functools.partial(sent, plane, plane.at[0:31], s_pla))
    wait_all(dpool, r_dp)
    wait_all(spill_back, r_last)
    wait_all(plane, r_pla)
    for wait in pending:
        wait()


def finish(starts, lengths, dpool, spill_back, inverse_before, out_in, plane, grad, patch_out, gq, gk):
    base = lax.axis_index("seq") * 128
    start = starts[...] - base
    length = lengths[...]
    at_byte = lax.broadcasted_iota(jnp.int32, (128, PIECE), 0)
    inside = (at_byte >= start) & (at_byte < start + length)
    member = inside.astype(f32).astype(bf16)
    by_byte = jnp.sum(jnp.where(inside, 1.0 / length.astype(f32), 0.0), 1, keepdims=True)
    lead = lax.broadcasted_iota(jnp.int32, (8, 1), 0) < start[:, 0:1]
    grad[...] = jnp.dot(member, dpool[...], preferred_element_type=f32) * by_byte
    grad[0:8, :] = jnp.where(lead, spill_back[...] * inverse_before[:, 0:1], grad[0:8, :])
    patch_out[...] = out_in[...]

    @pl.when(pl.program_id(0) == 0)
    def _():
        for i in range(HEADS):
            gq[i:i + 1, :] = plane[i, 0:1, :]
            gk[i:i + 1, :] = plane[i, 1:2, :]


VMEM = pl.BlockSpec(memory_space=pltpu.VMEM)
ANY = pl.BlockSpec(memory_space=pl.ANY)
DMA = pltpu.SemaphoreType.DMA
PARTS = 4


def shape(dims, dtype):
    return jax.ShapeDtypeStruct(dims, dtype)


def on_device(byte_states, patch_starts, patch_lengths, query_gain, key_gain, out_cotangent):
    states = byte_states[0]
    cot = out_cotangent[0]
    width = states.shape[1]
    own = 2 * BLOCK
    keys = 8 * BLOCK
    V = pltpu.VMEM
    out_rows, dpool, spill_back, plane, inverse_before = pl.pallas_call(
        whole,
        out_shape=(shape((PIECE, width), bf16), shape((PIECE, width), bf16), shape((1, width), f32),
                   shape((HEADS, 2, HEAD_DIM), f32), shape((1, HEAD_DIM), f32)),
        in_specs=[ANY, VMEM, VMEM, VMEM, VMEM, ANY],
        out_specs=(VMEM,) * 5,
        scratch_shapes=[
            V((128, width), bf16), V((PIECE, width), bf16), V((PIECE, width), bf16), V((PIECE, width), f32),
            V((1, width), f32), V((1, width), f32), V((1, HEAD_DIM), f32),
            V((128, PIECE, HEAD_DIM), bf16), V((own, HEAD_DIM), bf16), V((own, HEAD_DIM), bf16),
            V((keys, HEAD_DIM), bf16), V((own, HEAD_DIM), bf16),
            V((BLOCK, STEPS * BLOCK), f32), V((BLOCK, STEPS * BLOCK), bf16), V((BLOCK, STEPS * BLOCK), f32),
            V((keys, HEAD_DIM), f32), V((keys, HEAD_DIM), f32),
            V((own, HEAD_DIM), f32), V((own, HEAD_DIM), f32), V((own, HEAD_DIM), f32), V((own, HEAD_DIM), f32),
            V((own, HEAD_DIM), bf16),
            V((4, BLOCK, HEAD_DIM), f32), V((2, BLOCK, HEAD_DIM), bf16), V((2, BLOCK, HEAD_DIM), bf16),
            V((own, HEAD_DIM), bf16), V((HEADS, 1, HEAD_DIM), f32), V((8, 2, HEAD_DIM), f32),
            DMA((2,)), DMA, DMA, DMA((2,)), DMA((2,)), DMA, DMA, DMA((12,)), DMA((12,)),
            DMA, DMA, DMA((4,)), DMA((4,)), DMA((2,)), DMA((2,)), DMA, DMA, DMA, DMA, DMA, DMA,
            DMA, DMA, DMA, DMA,
        ],
        compiler_params=pltpu.CompilerParams(
            collective_id=0, has_side_effects=True, vmem_limit_bytes=56 << 20
        ),
    )(states, patch_starts, patch_lengths, query_gain.reshape(HEADS, HEAD_DIM), key_gain.reshape(HEADS, HEAD_DIM), cot)
    part = width // PARTS

    def columns(rows):
        return pl.BlockSpec((rows, part), lambda i: (0, i))

    grad, patch_out, gq, gk = pl.pallas_call(
        finish,
        grid=(PARTS,),
        out_shape=(shape((128, width), f32), shape((PIECE, width), bf16),
                   shape((HEADS, HEAD_DIM), f32), shape((HEADS, HEAD_DIM), f32)),
        in_specs=[VMEM, VMEM, columns(PIECE), columns(1), VMEM, columns(PIECE), VMEM],
        out_specs=(columns(128), columns(PIECE), VMEM, VMEM),
        compiler_params=pltpu.CompilerParams(vmem_limit_bytes=62 << 20),
    )(patch_starts, patch_lengths, dpool, spill_back, inverse_before, out_rows, plane)
    return patch_out[None], grad[None], gq.reshape(width), gk.reshape(width)


def solution(mesh):
    rows = P("dp", "seq", None)
    flat = P("dp", "seq")
    return jax.shard_map(
        on_device,
        mesh=mesh,
        in_specs=(rows, flat, flat, P(), P(), rows),
        out_specs=(rows, rows, P(), P()),
        check_vma=False,
    )
```

time: 79.2 us -> 69.6 us (0.88)
  Pallas kernels: 73.5 us -> 68.6 us
  local copies, waits for them, and re-layouts: 4.68 us -> 0 us
    pallas_call x1, Pallas kernels: 71.1 us -> 64.7 us  [on_device(): pl.pallas_call(whole, out_shape=(shape((PIECE, width), bf16), shape((PIEC...]
    unnamed x12 -> x0, local copies, waits for them, and re-layouts: 4.68 us -> none
    pallas_call x1, Pallas kernels: 2.37 us -> 3.85 us  [on_device(): pl.pallas_call(finish, grid=(PARTS,), out_shape=(shape((128, width), f32)...]
where the time goes in v3:
time: 69.6 us; the launch traced here: 69.2 us
  Pallas kernels  68.6 us (99%)
    pallas_call x1, Pallas kernels, on_device(): pl.pallas_call(whole, out_shape=(shape((PIECE, width), bf16), shape((PIEC...  64.7 us
    pallas_call x1, Pallas kernels, on_device(): pl.pallas_call(finish, grid=(PARTS,), out_shape=(shape((128, width), f32)...  3.85 us

profile of v3, /device:TPU:1, one launch (start us, length us, event | category | flops | bytes accessed | tf_op | source)
XLA Modules:
  0.0 69.2 jit_solution(18210146828742304723)
XLA Ops:
  0.6 64.7 %shard_map.93 = (bf16[32,4096]{1,0:T(8,128)(2,1)}, bf16[32,4096]{1,0:T(8,128)(2,1)}, f32[1,4096]{1,0:T(1,128)}, f32[32,2,128]{2,1,0:T(2,128)}, f32[1,128]{1,0:T(1,128)}) custom-call(bf16[128,4096]{1,0:T(8,128)(2,1)} %bitcast.8, s32[1,32]{1,0:T(1,128)} %starts.3, s32[1,32]{1,0:T(1,128)} %lengths.3, f32[32,128]{1,0:T(8,128)} %bitcast.10, f32[32,128]{1,0:T(8,128)} %bitcast.11, ...), custom_call_target="tpu_custom_call" | custom-call | tf_op jit(solution)/shard_map/pallas_call | solution.py:516
  65.4 3.8 %shard_map.94 = (f32[128,4096]{1,0:T(8,128)}, bf16[32,4096]{1,0:T(8,128)(2,1)}, f32[32,128]{1,0:T(8,128)}, f32[32,128]{1,0:T(8,128)}) custom-call(s32[1,32]{1,0:T(1,128)} %starts.3, s32[1,32]{1,0:T(1,128)} %lengths.3, bf16[32,4096]{1,0:T(8,128)(2,1)} %get-tuple-element.13.dpool, f32[1,4096]{1,0:T(1,128)} %get-tuple-element.14.spill_back, ...), custom_call_target="tpu_custom_call" | custom-call | tf_op jit(solution)/shard_map/pallas_call | solution.py:546

commit v4 on v3

--- a/solution.py
+++ b/solution.py
@@ -168,37 +168,59 @@
     def cols(t):
         return pl.ds(pl.multiple_of(t * BLOCK, BLOCK), BLOCK)
 
+    def dvalue(t, high, j):
+        dv[chunk(j), :] += lax.dot_general(w_ref[:, cols(t)], dmb[chunk(high), :], TN, preferred_element_type=f32)
+
     delta[...] = jnp.zeros(delta.shape, f32)
 
-    def dprobs(steps):
+    def dprobs(steps, far):
         for t in steps:
             high, j = step_at(low, t)
             dp = lax.dot_general(dmb[chunk(high), :], values(j), NT, preferred_element_type=f32)
             d_ref[:, cols(t)] = dp
-            dv[chunk(j), :] += lax.dot_general(w_ref[:, cols(t)], dmb[chunk(high), :], TN, preferred_element_type=f32)
             delta[chunk(high), :] += lanes(dp * s_ref[:, cols(t)], jnp.add)
-
-    over_steps(dprobs)
+            if far:
+                dvalue(t, high, j)
+
+    dprobs((0, 8, 7), False)
+    dprobs((5, 6), False)
+    dprobs((1, 3), True)
+    dprobs((2, 4), True)
     delta[...] = jnp.broadcast_to(jnp.sum(delta[...], -1, keepdims=True), delta.shape) * stat[...]
     stat[...] = stat[...] * SCALE
     dq[...] = jnp.zeros(dq.shape, f32)
 
-    def back(steps):
+    def dquery(ds, high, j):
+        dq[chunk(high), :] += jnp.dot(ds, keyed[chunk(j), :], preferred_element_type=f32)
+
+    def back(steps, far):
         for t in steps:
             high, j = step_at(low, t)
             ds = ((s_ref[:, cols(t)] * tiled(stat[chunk(high), :]))
                   * (d_ref[:, cols(t)] - tiled(delta[chunk(high), :]))).astype(bf16)
+            if not far:
+                dvalue(t, high, j)
             dk[chunk(j), :] += lax.dot_general(ds, query[chunk(high), :], TN, preferred_element_type=f32)
-            dq[chunk(high), :] += jnp.dot(ds, keyed[chunk(j), :], preferred_element_type=f32)
-
-    for n, steps in enumerate(((1, 2), (3, 4), (5, 6), (0, 8, 7))):
-        back(steps)
-        after(n)
+            if far:
+                w_ref[:, cols(t)] = ds
+            else:
+                dquery(ds, high, j)
+
+    back((1, 3), True)
+    after(0)
+    back((2, 4), True)
+    after(1)
+    back((5, 6), False)
+    after(2)
+    for t in (1, 2, 3, 4):
+        dquery(w_ref[:, cols(t)], *step_at(low, t))
+    back((0, 8, 7), False)
+    after(3)
 
 
 def whole(states, starts, lengths, qgain_all, kgain_all, cot_rows,
           patch_out, dpool, spill_back, plane, inverse_before,
-          bytes_in, cot, pooled, sums, spill, spill_in, inverse_out, kfull, cot_h, out_h,
+          bytes_in, cot_in, cot, pooled, sums, spill, spill_in, inverse_out, kfull, cot_h, out_h,
           keyed, query, s_ref, w_ref, d_ref, dk, dv, dq, stat, delta, mixed, dmb,
           from_sib, to_far, from_far, mine_b, last_rows, column_in,
           s_load, s_spill, r_spill, s_pool, r_pool, s_cot, r_cot, s_key, r_key,
@@ -232,11 +254,13 @@
             wait_all(ref, sem)
 
     load_bytes = pltpu.make_async_copy(states, bytes_in, s_load.at[0])
-    load_cot = pltpu.make_async_copy(cot_rows, cot, s_load.at[1])
+    load_cot = pltpu.make_async_copy(cot_rows, cot_in, s_load.at[1])
     load_bytes.start()
     load_cot.start()
 
     barrier = pltpu.get_barrier_semaphore()
+    signal(barrier, before, core)
+    signal(barrier, after, core)
 
     def greet(i, _):
         s, d, _row = source(y, core, (i + head) % 32)
@@ -255,8 +279,6 @@
         return 0
 
     lax.fori_loop(1, 8, greet_column, 0)
-    signal(barrier, after, core)
-    signal(barrier, before, core)
 
     base = seq * 128
     start = column(starts[...], PIECE) - base
@@ -288,7 +310,7 @@
     def scatter_rows(src, dst, first_row, count, send, recv):
         def step(i, _):
             h = head_at(x, z, i)
-            part = src.at[pl.ds(first_row, count), pl.ds(pl.multiple_of(h * HEAD_DIM, HEAD_DIM), HEAD_DIM)]
+            part = src.at[h, pl.ds(first_row, count), :]
             target = oy * 32 + h
             local = (target == seq) & (ocore == core)
 
@@ -304,20 +326,19 @@
 
         lax.fori_loop(0, 32, step, 0)
 
-    columns = pl.ds(0, 31 * HEAD_DIM)
-    pooled[0:16, :] = sums[0:16, :].astype(bf16)
+    def by_head(ref, first_row, value):
+        for h in range(HEADS):
+            ref[h, first_row:first_row + value.shape[0], :] = value[:, h * HEAD_DIM:(h + 1) * HEAD_DIM]
+
+    by_head(pooled, 0, sums[0:16, :].astype(bf16))
     scatter_rows(pooled, kfull.at[seq, pl.ds(0, 16), :], 0, 16, s_pool.at[0], r_pool.at[0])
     spilling.wait_recv()
     last = (lax.broadcasted_iota(jnp.int32, (16, 1), 0) == 15) & (seq < 127)
-    pooled[16:32, :] = (sums[16:32, :] + jnp.where(last, spill_in[...] * inverse[16:32, :], 0.0)).astype(bf16)
+    by_head(pooled, 16, (sums[16:32, :] + jnp.where(last, spill_in[...] * inverse[16:32, :], 0.0)).astype(bf16))
     scatter_rows(pooled, kfull.at[seq, pl.ds(16, 16), :], 16, 16, s_pool.at[1], r_pool.at[1])
-    load_cot.wait()
-    crow = pl.multiple_of(ohigh * BLOCK + (seq % 16) * PIECE, PIECE)
-    scatter_rows(cot, cot_h.at[pl.ds(crow, PIECE), :], 0, PIECE, s_cot, r_cot)
     for i in range(2):
-        half = pooled.at[pl.ds(16 * i, 16), :]
-        pending.append(functools.partial(sent, half, half.at[:, columns], s_pool.at[i]))
-    pending.append(functools.partial(sent, cot, cot.at[:, columns], s_cot))
+        half = pl.ds(16 * i, 16)
+        pending.append(functools.partial(sent, pooled.at[:, half, :], pooled.at[0:31, half, :], s_pool.at[i]))
 
     qgain = qgain_all[pl.ds(head, 1), :]
     kgain = kgain_all[pl.ds(head, 1), :]
@@ -328,6 +349,9 @@
         return 0
 
     lax.fori_loop(0, 8, clear, 0)
+    load_cot.wait()
+    by_head(cot, 0, cot_in[...])
+    crow = pl.multiple_of(ohigh * BLOCK + (seq % 16) * PIECE, PIECE)
 
     def pieces(block):
         return pl.ds(block * 16, 16)
@@ -350,6 +374,8 @@
             beside[n] = remote(there, there, s_key.at[4 + n], r_key.at[4 + n], seq, 1 - core)
             beside[n].start()
             pending.extend([across[n].wait_send, beside[n].wait_send])
+    scatter_rows(cot, cot_h.at[pl.ds(crow, PIECE), :], 0, PIECE, s_cot, r_cot)
+    pending.append(functools.partial(sent, cot, cot.at[0:31], s_cot))
     for i, block in enumerate((low, 7 - low)):
         query[chunk(i), :] = (values(block).astype(f32) * qgain).astype(bf16)
         prepare(block)
@@ -398,7 +424,7 @@
     def rows_of(ref):
         return lambda n: ref.at[pl.ds(pl.multiple_of(n * PIECE, PIECE), PIECE), :]
 
-    scatter_back(0, 32, rows_of(out_h), patch_out.at[:, head_columns], s_out, r_out)
+    scatter_back(0, 32, rows_of(out_h), patch_out.at[head], s_out, r_out)
     pending.append(functools.partial(sent, out_h, out_h.at[0:31 * PIECE], s_out))
     pending.append(functools.partial(wait_all, patch_out, r_out))
     wait_all(cot_h, r_cot)
@@ -420,34 +446,32 @@
         to_sib[i].start()
         pending.append(to_sib[i].wait_send)
 
+    outer = 1 - low // 2
+
+    def in_turn(block, turn):
+        return block + ((turn + outer + 1) % 2) * (7 - 2 * block)
+
+    def combine(turn):
+        to_sib[turn].wait_recv()
+        to_far[turn] = (dv[chunk(in_turn(far, turn)), :] + from_sib[turn]).astype(bf16)
+        to_partner.append(remote(to_far.at[turn], from_far.at[turn], s_far.at[turn], r_far.at[turn], partner, core))
+        to_partner[turn].start()
+        pending.append(to_partner[turn].wait_send)
+
     def after_steps(n):
-        blocks = ((farsib, 7 - farsib), (far, 7 - far), (sib, 7 - sib), (low, 7 - low))[n]
-        for i, block in enumerate(blocks):
-            complete(block)
-            if n in (0, 2):
-                give_sib(block)
-            if n == 1:
-                to_sib[i].wait_recv()
-                to_far[i] = (dv[chunk(block), :] + from_sib[i]).astype(bf16)
-                to_partner.append(remote(to_far.at[i], from_far.at[i], s_far.at[i], r_far.at[i], partner, core))
-                to_partner[i].start()
-                pending.append(to_partner[i].wait_send)
+        if n < 2:
+            complete(in_turn(farsib, n))
+            give_sib(in_turn(farsib, n))
+            complete(in_turn(far, n))
+        else:
+            for block in ((sib, 7 - sib), (low, 7 - low))[n - 2]:
+                complete(block)
+                if n == 2:
+                    give_sib(block)
+        if n in (1, 2):
+            combine(n - 1)
 
     backward(low, values, keyed, query, dmb, s_ref, w_ref, d_ref, stat, delta, dk, dv, dq, after_steps)
-    for i, block in enumerate((low, 7 - low)):
-        to_sib[2 + i].wait_recv()
-        to_partner[i].wait_recv()
-        mixed[chunk(i), :] = (dv[chunk(block), :] + from_sib[2 + i] + dq[chunk(i), :] * qgain
-                              + from_far[i].astype(f32))
-        mine_b[chunk(i), :] = mixed[chunk(i), :].astype(bf16)
-        scatter_back(16 * i, 16, rows_of(mine_b), dpool.at[:, head_columns], s_dp, r_dp)
-    pending.append(functools.partial(sent, mine_b, mine_b.at[0:31 * PIECE], s_dp))
-
-    for i in range(32):
-        last_rows[i] = mixed[i * PIECE + PIECE - 1:(i + 1) * PIECE, :]
-    scatter_back(0, 32, lambda n: last_rows.at[n], spill_back.at[:, head_columns], s_last, r_last, 1)
-    pending.append(functools.partial(sent, last_rows, last_rows.at[0:31], s_last, mine_before))
-
     gq = jnp.zeros((1, HEAD_DIM), f32)
     for i, block in enumerate((low, 7 - low)):
         gq = gq + jnp.sum(dq[chunk(i), :] * values(block).astype(f32), 0, keepdims=True)
@@ -461,13 +485,29 @@
         return 0
 
     lax.fori_loop(1, 8, send_column, 0)
-    wait_all(column_in.at[0:7], r_col)
-    total = column_in[0]
-    for i in range(1, 8):
-        total = total + column_in[i]
-    wait_all(column_in.at[0:7], s_col)
-    column_in[place_in_column] = total[None]
-    scatter_back(0, 32, lambda n: column_in.at[y * 2 + core], plane.at[head], s_pla, r_pla)
+    to_sib[2].wait_recv()
+    to_sib[3].wait_recv()
+    for turn in range(2):
+        high = (turn + outer) % 2
+        mixed[chunk(high), :] = (dv[chunk(low + high * (7 - 2 * low)), :] + from_sib[2 + high]
+                                 + dq[chunk(high), :] * qgain)
+        to_partner[turn].wait_recv()
+        mixed[chunk(high), :] += from_far[turn].astype(f32)
+        mine_b[chunk(high), :] = mixed[chunk(high), :].astype(bf16)
+        scatter_back(16 * high, 16, rows_of(mine_b), dpool.at[head], s_dp, r_dp)
+        for i in range(16):
+            last_rows[16 * high + i] = mixed[pl.ds(high * BLOCK + i * PIECE + PIECE - 1, 1), :]
+        scatter_back(16 * high, 16, lambda n: last_rows.at[n], spill_back.at[:, head_columns], s_last, r_last, 1)
+        if turn == 0:
+            wait_all(column_in.at[0:7], r_col)
+            total = column_in[0]
+            for i in range(1, 8):
+                total = total + column_in[i]
+            wait_all(column_in.at[0:7], s_col)
+            column_in[place_in_column] = total[None]
+            scatter_back(0, 32, lambda n: column_in.at[y * 2 + core], plane.at[head], s_pla, r_pla)
+    pending.append(functools.partial(sent, mine_b, mine_b.at[0:31 * PIECE], s_dp))
+    pending.append(functools.partial(sent, last_rows, last_rows.at[0:31], s_last, mine_before))
     pending.append(functools.partial(sent, plane, plane.at[0:31], s_pla))
     wait_all(dpool, r_dp)
     wait_all(spill_back, r_last)
@@ -476,24 +516,55 @@
         wait()
 
 
-def finish(starts, lengths, dpool, spill_back, inverse_before, out_in, plane, grad, patch_out, gq, gk):
+def finish(starts, lengths, dpool, spill_back, inverse_before, out_in, plane, grad, patch_out, gq, gk,
+           starts_v, lengths_v, dpool_v, spill_v, inverse_v, out_v, plane_v, grad_v, rows_v, gains_v, s_in, s_to):
+    loads = []
+    for n, (src, dst) in enumerate(((starts, starts_v), (lengths, lengths_v), (spill_back, spill_v),
+                                    (inverse_before, inverse_v), (out_in, out_v), (plane, plane_v))):
+        loads.append(pltpu.make_async_copy(src, dst, s_in.at[n]))
+    each = HEADS // PARTS
+    parts = []
+    for p in range(PARTS):
+        heads = pl.ds(p * each, each)
+        parts.append(pltpu.make_async_copy(dpool.at[heads], dpool_v.at[heads], s_in.at[len(loads) + p]))
+    for copy in loads[:4] + parts + loads[4:]:
+        copy.start()
+    for copy in loads[:4]:
+        copy.wait()
     base = lax.axis_index("seq") * 128
-    start = starts[...] - base
-    length = lengths[...]
+    start = starts_v[...] - base
+    length = lengths_v[...]
     at_byte = lax.broadcasted_iota(jnp.int32, (128, PIECE), 0)
     inside = (at_byte >= start) & (at_byte < start + length)
     member = inside.astype(f32).astype(bf16)
     by_byte = jnp.sum(jnp.where(inside, 1.0 / length.astype(f32), 0.0), 1, keepdims=True)
     lead = lax.broadcasted_iota(jnp.int32, (8, 1), 0) < start[:, 0:1]
-    grad[...] = jnp.dot(member, dpool[...], preferred_element_type=f32) * by_byte
-    grad[0:8, :] = jnp.where(lead, spill_back[...] * inverse_before[:, 0:1], grad[0:8, :])
-    patch_out[...] = out_in[...]
-
-    @pl.when(pl.program_id(0) == 0)
-    def _():
-        for i in range(HEADS):
-            gq[i:i + 1, :] = plane[i, 0:1, :]
-            gk[i:i + 1, :] = plane[i, 1:2, :]
+    stores = []
+
+    def store(src, dst):
+        stores.append(pltpu.make_async_copy(src, dst, s_to.at[len(stores)]))
+        stores[-1].start()
+
+    for p in range(PARTS):
+        parts[p].wait()
+        for h in range(p * each, (p + 1) * each):
+            columns = slice(h * HEAD_DIM, (h + 1) * HEAD_DIM)
+            grad_v[:, columns] = jnp.dot(member, dpool_v[h], preferred_element_type=f32) * by_byte
+            grad_v[0:8, columns] = jnp.where(lead, spill_v[:, columns] * inverse_v[...], grad_v[0:8, columns])
+        columns = pl.ds(p * each * HEAD_DIM, each * HEAD_DIM)
+        store(grad_v.at[:, columns], grad.at[:, columns])
+    loads[4].wait()
+    for h in range(HEADS):
+        rows_v[:, h * HEAD_DIM:(h + 1) * HEAD_DIM] = out_v[h]
+    store(rows_v, patch_out)
+    loads[5].wait()
+    for h in range(HEADS):
+        for i in range(2):
+            gains_v[i, h:h + 1, :] = plane_v[h, i:i + 1, :]
+    store(gains_v.at[0], gq)
+    store(gains_v.at[1], gk)
+    for copy in stores:
+        copy.wait()
 
 
 VMEM = pl.BlockSpec(memory_space=pltpu.VMEM)
@@ -512,15 +583,16 @@
     width = states.shape[1]
     own = 2 * BLOCK
     keys = 8 * BLOCK
+    by_head = (HEADS, PIECE, HEAD_DIM)
     V = pltpu.VMEM
     out_rows, dpool, spill_back, plane, inverse_before = pl.pallas_call(
         whole,
-        out_shape=(shape((PIECE, width), bf16), shape((PIECE, width), bf16), shape((1, width), f32),
+        out_shape=(shape(by_head, bf16), shape(by_head, bf16), shape((1, width), f32),
                    shape((HEADS, 2, HEAD_DIM), f32), shape((1, HEAD_DIM), f32)),
         in_specs=[ANY, VMEM, VMEM, VMEM, VMEM, ANY],
-        out_specs=(VMEM,) * 5,
+        out_specs=(ANY,) * 5,
         scratch_shapes=[
-            V((128, width), bf16), V((PIECE, width), bf16), V((PIECE, width), bf16), V((PIECE, width), f32),
+            V((128, width), bf16), V((PIECE, width), bf16), V(by_head, bf16), V(by_head, bf16), V((PIECE, width), f32),
             V((1, width), f32), V((1, width), f32), V((1, HEAD_DIM), f32),
             V((128, PIECE, HEAD_DIM), bf16), V((own, HEAD_DIM), bf16), V((own, HEAD_DIM), bf16),
             V((keys, HEAD_DIM), bf16), V((own, HEAD_DIM), bf16),
@@ -538,18 +610,17 @@
             collective_id=0, has_side_effects=True, vmem_limit_bytes=56 << 20
         ),
     )(states, patch_starts, patch_lengths, query_gain.reshape(HEADS, HEAD_DIM), key_gain.reshape(HEADS, HEAD_DIM), cot)
-    part = width // PARTS
-
-    def columns(rows):
-        return pl.BlockSpec((rows, part), lambda i: (0, i))
-
     grad, patch_out, gq, gk = pl.pallas_call(
         finish,
-        grid=(PARTS,),
         out_shape=(shape((128, width), f32), shape((PIECE, width), bf16),
                    shape((HEADS, HEAD_DIM), f32), shape((HEADS, HEAD_DIM), f32)),
-        in_specs=[VMEM, VMEM, columns(PIECE), columns(1), VMEM, columns(PIECE), VMEM],
-        out_specs=(columns(128), columns(PIECE), VMEM, VMEM),
+        in_specs=[ANY] * 7,
+        out_specs=(ANY,) * 4,
+        scratch_shapes=[
+            V((1, PIECE), jnp.int32), V((1, PIECE), jnp.int32), V(by_head, bf16), V((1, width), f32),
+            V((1, HEAD_DIM), f32), V(by_head, bf16), V((HEADS, 2, HEAD_DIM), f32), V((128, width), f32),
+            V((PIECE, width), bf16), V((2, HEADS, HEAD_DIM), f32), DMA((6 + PARTS,)), DMA((3 + PARTS,)),
+        ],
         compiler_params=pltpu.CompilerParams(vmem_limit_bytes=62 << 20),
     )(patch_starts, patch_lengths, dpool, spill_back, inverse_before, out_rows, plane)
     return patch_out[None], grad[None], gq.reshape(width), gk.reshape(width)

time: 69.6 us -> 62.9 us (0.904)
  Pallas kernels: 68.6 us -> 62.1 us
    pallas_call x2, Pallas kernels: 68.6 us -> 62.1 us  [the longest x1 59.4 us: on_device(): pl.pallas_call(whole, out_shape=(shape(by_head, bf16), shape(by_head, bf1...]
where the time goes in v4:
time: 62.9 us; the launch traced here: 62.8 us
  Pallas kernels  62.1 us (99%)
  between operations  0.64 us (1%)
    pallas_call x1, Pallas kernels, on_device(): pl.pallas_call(whole, out_shape=(shape(by_head, bf16), shape(by_head, bf1...  59.4 us
    pallas_call x1, Pallas kernels, on_device(): pl.pallas_call(finish, out_shape=(shape((128, width), f32), shape((PIECE,...  2.75 us

profile of v4, /device:TPU:1, one launch (start us, length us, event | category | flops | bytes accessed | tf_op | source)
XLA Modules:
  0.0 62.8 jit_solution(10900084252340518071)
XLA Ops:
  0.6 59.4 %shard_map.93 = (bf16[32,32,128]{2,1,0:T(8,128)(2,1)}, bf16[32,32,128]{2,1,0:T(8,128)(2,1)}, f32[1,4096]{1,0:T(1,128)}, f32[32,2,128]{2,1,0:T(2,128)}, f32[1,128]{1,0:T(1,128)}) custom-call(bf16[128,4096]{1,0:T(8,128)(2,1)} %bitcast.8, s32[1,32]{1,0:T(1,128)} %starts.3, s32[1,32]{1,0:T(1,128)} %lengths.3, f32[32,128]{1,0:T(8,128)} %bitcast.10, ...), custom_call_target="tpu_custom_call" | custom-call | tf_op jit(solution)/shard_map/pallas_call | solution.py:588
  60.0 2.8 %shard_map.94 = (f32[128,4096]{1,0:T(8,128)}, bf16[32,4096]{1,0:T(8,128)(2,1)}, f32[32,128]{1,0:T(8,128)}, f32[32,128]{1,0:T(8,128)}) custom-call(s32[1,32]{1,0:T(1,128)} %starts.3, s32[1,32]{1,0:T(1,128)} %lengths.3, bf16[32,32,128]{2,1,0:T(8,128)(2,1)} %get-tuple-element.13.dpool, f32[1,4096]{1,0:T(1,128)} %get-tuple-element.14.spill_back, ...), custom_call_target="tpu_custom_call" | custom-call | tf_op jit(solution)/shard_map/pallas_call | solution.py:613

commit v5 on v4

--- a/solution.py
+++ b/solution.py
@@ -99,62 +99,68 @@
     return 1 - second + mirrored, chunk_low + mirrored * (7 - 2 * chunk_low)
 
 
-def over_steps(body, between=None):
-    body((0, 8, 7))
-    if between is not None:
-        between()
-
-    def three(i, _):
-        body(tuple(1 + 3 * i + u for u in range(3)))
-        return 0
-
-    lax.fori_loop(0, 2, three, 0)
+def group(t):
+    return 1 if t in (1, 2, 3, 4) else 0
 
 
 def tiled(x):
     return jnp.concatenate([x] * GROUP, 1)
 
 
-def forward(low, values, keyed, query, s_ref, w_ref, stat, mixed, between):
+def forward(low, values, keyed, query, s_ref, w_ref, stat, delta, mixed, early, sib_keys, far_keys, farsib_keys):
+    def cols(t):
+        return pl.ds(t * BLOCK, BLOCK)
+
     stat[...] = jnp.full(stat.shape, -1e30, f32)
-
-    def cols(t):
-        return pl.ds(pl.multiple_of(t * BLOCK, BLOCK), BLOCK)
+    delta[...] = jnp.zeros(delta.shape, f32)
+    mixed[...] = jnp.zeros(mixed.shape, f32)
 
     def scores(steps):
         for t in steps:
             high, j = step_at(low, t)
             s = lax.dot_general(query[chunk(high), :], keyed[chunk(j), :], NT, preferred_element_type=f32)
-            if isinstance(t, int) and t != 7:
+            if t in (0, 8):
                 r = lax.broadcasted_iota(jnp.int32, s.shape, 0)
                 c = lax.broadcasted_iota(jnp.int32, s.shape, 1)
                 s = jnp.where(c <= r, s, -1e30)
             s_ref[:, cols(t)] = s
-            stat[chunk(high), :] = jnp.maximum(stat[chunk(high), :], lanes(s, jnp.maximum))
-
-    over_steps(scores, between)
-    stat[...] = jnp.broadcast_to(jnp.max(stat[...], -1, keepdims=True), stat.shape)
-    mixed[...] = jnp.zeros(mixed.shape, f32)
+            here = stat.at[group(t), chunk(high), :]
+            here[...] = jnp.maximum(here[...], lanes(s, jnp.maximum))
 
     def expo(steps):
+        g = group(steps[0])
+        stat[g] = jnp.broadcast_to(jnp.max(stat[g], -1, keepdims=True), stat.shape[1:])
         for t in steps:
             high, j = step_at(low, t)
-            e = jnp.exp2((s_ref[:, cols(t)] - tiled(stat[chunk(high), :])) * C2)
+            e = jnp.exp2((s_ref[:, cols(t)] - tiled(stat[g, chunk(high), :])) * C2)
             s_ref[:, cols(t)] = e
-            mixed[chunk(high), :] += lanes(e, jnp.add)
-
-    over_steps(expo)
-    stat[...] = jnp.broadcast_to(1.0 / jnp.sum(mixed[...], -1, keepdims=True), stat.shape)
-    mixed[...] = jnp.zeros(mixed.shape, f32)
+            delta[g, chunk(high), :] += lanes(e, jnp.add)
+
+    scores((0, 8, 7))
+    early()
+    sib_keys()
+    scores((5, 6))
+    expo((0, 8, 7, 5, 6))
+    far_keys()
+    scores((3, 4))
+    farsib_keys()
+    scores((1, 2))
+    expo((3, 4, 1, 2))
+    top = jnp.maximum(stat[0], stat[1])
+    parts = [jnp.exp2((stat[g] - top) * C2) for g in range(2)]
+    total = sum(parts[g] * jnp.sum(delta[g], -1, keepdims=True) for g in range(2))
+    for g in range(2):
+        stat[g] = parts[g] / total
 
     def mix(steps):
         for t in steps:
             high, j = step_at(low, t)
-            w = (s_ref[:, cols(t)] * tiled(stat[chunk(high), :])).astype(bf16)
+            w = (s_ref[:, cols(t)] * tiled(stat[group(t), chunk(high), :])).astype(bf16)
             w_ref[:, cols(t)] = w
             mixed[chunk(high), :] += jnp.dot(w, values(j), preferred_element_type=f32)
 
-    over_steps(mix)
+    for steps in ((0, 8, 7), (5, 6, 3), (4, 1, 2)):
+        mix(steps)
 
 
 def normed(mixed, out):
@@ -166,27 +172,24 @@
 
 def backward(low, values, keyed, query, dmb, s_ref, w_ref, d_ref, stat, delta, dk, dv, dq, after):
     def cols(t):
-        return pl.ds(pl.multiple_of(t * BLOCK, BLOCK), BLOCK)
+        return pl.ds(t * BLOCK, BLOCK)
 
     def dvalue(t, high, j):
         dv[chunk(j), :] += lax.dot_general(w_ref[:, cols(t)], dmb[chunk(high), :], TN, preferred_element_type=f32)
 
     delta[...] = jnp.zeros(delta.shape, f32)
 
-    def dprobs(steps, far):
+    def dprobs(steps):
         for t in steps:
             high, j = step_at(low, t)
             dp = lax.dot_general(dmb[chunk(high), :], values(j), NT, preferred_element_type=f32)
             d_ref[:, cols(t)] = dp
-            delta[chunk(high), :] += lanes(dp * s_ref[:, cols(t)], jnp.add)
-            if far:
-                dvalue(t, high, j)
-
-    dprobs((0, 8, 7), False)
-    dprobs((5, 6), False)
-    dprobs((1, 3), True)
-    dprobs((2, 4), True)
-    delta[...] = jnp.broadcast_to(jnp.sum(delta[...], -1, keepdims=True), delta.shape) * stat[...]
+            delta[group(t), chunk(high), :] += lanes(dp * s_ref[:, cols(t)], jnp.add)
+
+    for steps in ((0, 8, 7), (5, 6, 3), (4, 1, 2)):
+        dprobs(steps)
+    summed = sum(jnp.sum(delta[g], -1, keepdims=True) * stat[g] for g in range(2))
+    delta[0] = summed
     stat[...] = stat[...] * SCALE
     dq[...] = jnp.zeros(dq.shape, f32)
 
@@ -196,10 +199,9 @@
     def back(steps, far):
         for t in steps:
             high, j = step_at(low, t)
-            ds = ((s_ref[:, cols(t)] * tiled(stat[chunk(high), :]))
-                  * (d_ref[:, cols(t)] - tiled(delta[chunk(high), :]))).astype(bf16)
-            if not far:
-                dvalue(t, high, j)
+            ds = ((s_ref[:, cols(t)] * tiled(stat[group(t), chunk(high), :]))
+                  * (d_ref[:, cols(t)] - tiled(delta[0, chunk(high), :]))).astype(bf16)
+            dvalue(t, high, j)
             dk[chunk(j), :] += lax.dot_general(ds, query[chunk(high), :], TN, preferred_element_type=f32)
             if far:
                 w_ref[:, cols(t)] = ds
@@ -222,7 +224,7 @@
           patch_out, dpool, spill_back, plane, inverse_before,
           bytes_in, cot_in, cot, pooled, sums, spill, spill_in, inverse_out, kfull, cot_h, out_h,
           keyed, query, s_ref, w_ref, d_ref, dk, dv, dq, stat, delta, mixed, dmb,
-          from_sib, to_far, from_far, mine_b, last_rows, column_in,
+          from_sib, to_far, from_far, mine_b, last_rows, column_in, gains,
           s_load, s_spill, r_spill, s_pool, r_pool, s_cot, r_cot, s_key, r_key,
           s_out, r_out, s_sib, r_sib, s_far, r_far, s_dp, r_dp, s_col, r_col, s_pla, r_pla,
           s_last, r_last, s_inv, r_inv):
@@ -380,23 +382,36 @@
         query[chunk(i), :] = (values(block).astype(f32) * qgain).astype(bf16)
         prepare(block)
 
-    def other_keys():
+    def relay(n):
+        across[n].wait_recv()
+        there = kfull.at[pieces((far, 7 - far)[n % 2]), pl.ds(16 * (n // 2), 16), :]
+        relays[n] = remote(there, there, s_key.at[8 + n], r_key.at[8 + n], seq, 1 - core)
+        relays[n].start()
+        pending.append(relays[n].wait_send)
+
+    def early():
+        relay(0)
+        relay(1)
+
+    def sib_keys():
         for n in range(4):
-            block = (far, 7 - far)[n % 2]
-            across[n].wait_recv()
-            there = kfull.at[pieces(block), pl.ds(16 * (n // 2), 16), :]
-            relays[n] = remote(there, there, s_key.at[8 + n], r_key.at[8 + n], seq, 1 - core)
-            relays[n].start()
-            pending.append(relays[n].wait_send)
             beside[n].wait_recv()
-        for block in (sib, 7 - sib, far, 7 - far):
-            prepare(block)
+        prepare(sib)
+        prepare(7 - sib)
+
+    def far_keys():
+        relay(2)
+        relay(3)
+        prepare(far)
+        prepare(7 - far)
+
+    def farsib_keys():
         for n in range(4):
             relays[n].wait_recv()
-        for block in (farsib, 7 - farsib):
-            prepare(block)
-
-    forward(low, values, keyed, query, s_ref, w_ref, stat, mixed, other_keys)
+        prepare(farsib)
+        prepare(7 - farsib)
+
+    forward(low, values, keyed, query, s_ref, w_ref, stat, delta, mixed, early, sib_keys, far_keys, farsib_keys)
     rs = normed(mixed, out_h)
 
     head_columns = pl.ds(pl.multiple_of(head * HEAD_DIM, HEAD_DIM), HEAD_DIM)
@@ -503,15 +518,33 @@
             total = column_in[0]
             for i in range(1, 8):
                 total = total + column_in[i]
-            wait_all(column_in.at[0:7], s_col)
-            column_in[place_in_column] = total[None]
-            scatter_back(0, 32, lambda n: column_in.at[y * 2 + core], plane.at[head], s_pla, r_pla)
+            gains[pl.ds(head, 1)] = total[None]
+
+            def send_z(i, _):
+                slot = gains.at[pl.ds(head, 1)]
+                remote(slot, slot, s_pla.at[0], r_pla.at[0], y * 32 + x * 8 + (z + i) % 8, core).start()
+                return 0
+
+            lax.fori_loop(1, 8, send_z, 0)
+    wait_all(gains.at[0:7], r_pla.at[0])
+
+    def send_x(i, _):
+        slots = gains.at[pl.ds(x * 8, 8)]
+        remote(slots, slots, s_pla.at[1], r_pla.at[1], y * 32 + ((x + i) % 4) * 8 + z, core).start()
+        return 0
+
+    lax.fori_loop(1, 4, send_x, 0)
+    pending.append(functools.partial(wait_all, column_in.at[0:7], s_col))
+    pending.append(functools.partial(wait_all, gains.at[0:7], s_pla.at[0]))
+    pending.append(functools.partial(wait_all, gains.at[0:24], s_pla.at[1]))
     pending.append(functools.partial(sent, mine_b, mine_b.at[0:31 * PIECE], s_dp))
     pending.append(functools.partial(sent, last_rows, last_rows.at[0:31], s_last, mine_before))
-    pending.append(functools.partial(sent, plane, plane.at[0:31], s_pla))
+    wait_all(gains.at[0:24], r_pla.at[1])
+    store = pltpu.make_async_copy(gains, plane, s_load.at[0])
+    store.start()
     wait_all(dpool, r_dp)
     wait_all(spill_back, r_last)
-    wait_all(plane, r_pla)
+    store.wait()
     for wait in pending:
         wait()
 
@@ -598,12 +631,13 @@
             V((keys, HEAD_DIM), bf16), V((own, HEAD_DIM), bf16),
             V((BLOCK, STEPS * BLOCK), f32), V((BLOCK, STEPS * BLOCK), bf16), V((BLOCK, STEPS * BLOCK), f32),
             V((keys, HEAD_DIM), f32), V((keys, HEAD_DIM), f32),
-            V((own, HEAD_DIM), f32), V((own, HEAD_DIM), f32), V((own, HEAD_DIM), f32), V((own, HEAD_DIM), f32),
+            V((own, HEAD_DIM), f32), V((2, own, HEAD_DIM), f32), V((2, own, HEAD_DIM), f32), V((own, HEAD_DIM), f32),
             V((own, HEAD_DIM), bf16),
             V((4, BLOCK, HEAD_DIM), f32), V((2, BLOCK, HEAD_DIM), bf16), V((2, BLOCK, HEAD_DIM), bf16),
             V((own, HEAD_DIM), bf16), V((HEADS, 1, HEAD_DIM), f32), V((8, 2, HEAD_DIM), f32),
+            V((HEADS, 2, HEAD_DIM), f32),
             DMA((2,)), DMA, DMA, DMA((2,)), DMA((2,)), DMA, DMA, DMA((12,)), DMA((12,)),
-            DMA, DMA, DMA((4,)), DMA((4,)), DMA((2,)), DMA((2,)), DMA, DMA, DMA, DMA, DMA, DMA,
+            DMA, DMA, DMA((4,)), DMA((4,)), DMA((2,)), DMA((2,)), DMA, DMA, DMA, DMA, DMA((2,)), DMA((2,)),
             DMA, DMA, DMA, DMA,
         ],
         compiler_params=pltpu.CompilerParams(

time: 62.9 us -> 61.5 us (0.978)
  Pallas kernels: 62.1 us -> 60.5 us
    pallas_call x1, Pallas kernels: 59.4 us -> 57.7 us  [on_device(): pl.pallas_call(whole, out_shape=(shape(by_head, bf16), shape(by_head, bf1...]
where the time goes in v5:
time: 61.5 us; the launch traced here: 61.3 us
  Pallas kernels  60.5 us (98%)
  between operations  0.8 us (1%)
    pallas_call x1, Pallas kernels, on_device(): pl.pallas_call(whole, out_shape=(shape(by_head, bf16), shape(by_head, bf1...  57.7 us
    pallas_call x1, Pallas kernels, on_device(): pl.pallas_call(finish, out_shape=(shape((128, width), f32), shape((PIECE,...  2.75 us

profile of v5, /device:TPU:1, one launch (start us, length us, event | category | flops | bytes accessed | tf_op | source)
XLA Modules:
  0.0 61.3 jit_solution(551597736084007741)
XLA Ops:
  0.6 57.7 %shard_map.93 = (bf16[32,32,128]{2,1,0:T(8,128)(2,1)}, bf16[32,32,128]{2,1,0:T(8,128)(2,1)}, f32[1,4096]{1,0:T(1,128)}, f32[32,2,128]{2,1,0:T(2,128)}, f32[1,128]{1,0:T(1,128)}) custom-call(bf16[128,4096]{1,0:T(8,128)(2,1)} %bitcast.8, s32[1,32]{1,0:T(1,128)} %starts.3, s32[1,32]{1,0:T(1,128)} %lengths.3, f32[32,128]{1,0:T(8,128)} %bitcast.10, ...), custom_call_target="tpu_custom_call" | custom-call | tf_op jit(solution)/shard_map/pallas_call | solution.py:621
  58.4 2.7 %shard_map.94 = (f32[128,4096]{1,0:T(8,128)}, bf16[32,4096]{1,0:T(8,128)(2,1)}, f32[32,128]{1,0:T(8,128)}, f32[32,128]{1,0:T(8,128)}) custom-call(s32[1,32]{1,0:T(1,128)} %starts.3, s32[1,32]{1,0:T(1,128)} %lengths.3, bf16[32,32,128]{2,1,0:T(8,128)(2,1)} %get-tuple-element.13.dpool, f32[1,4096]{1,0:T(1,128)} %get-tuple-element.14.spill_back, ...), custom_call_target="tpu_custom_call" | custom-call | tf_op jit(solution)/shard_map/pallas_call | solution.py:647

commit v6 on v5

--- a/solution.py
+++ b/solution.py
@@ -88,15 +88,19 @@
     return functools.reduce(op, parts)
 
 
-def step_at(low, t):
-    if isinstance(t, int) and t in (0, 7, 8):
+def step_at(low, doc, t):
+    if t in (0, 7, 8):
         return {0: (0, low), 7: (1, low), 8: (1, 7 - low)}[t]
     mask = 3 - (t - 1) // 2
     second = (t - 1) % 2
-    odd, far = mask % 2, mask // 2
-    chunk_low = (low + odd) % 2 + 2 * ((low // 2 + far) % 2)
-    mirrored = second * (far * (1 - low // 2) + (1 - far) * (1 - low % 2))
-    return 1 - second + mirrored, chunk_low + mirrored * (7 - 2 * chunk_low)
+    chunk_low = (low + mask % 2) % 2 + 2 * ((low // 2 + mask // 2) % 2)
+    if t in (5, 6):
+        even = 1 - low % 2
+        high, mirrored = 1 - second * (1 - even), second * even
+    else:
+        outer = 1 - low // 2
+        high, mirrored = 1 - second * (1 - outer), outer * ((second + doc) % 2)
+    return high, chunk_low + mirrored * (7 - 2 * chunk_low)
 
 
 def group(t):
@@ -107,7 +111,7 @@
     return jnp.concatenate([x] * GROUP, 1)
 
 
-def forward(low, values, keyed, query, s_ref, w_ref, stat, delta, mixed, early, sib_keys, far_keys, farsib_keys):
+def forward(low, doc, values, keyed, query, s_ref, w_ref, stat, delta, mixed, early, sib_keys, far_keys, farsib_keys):
     def cols(t):
         return pl.ds(t * BLOCK, BLOCK)
 
@@ -117,7 +121,7 @@
 
     def scores(steps):
         for t in steps:
-            high, j = step_at(low, t)
+            high, j = step_at(low, doc, t)
             s = lax.dot_general(query[chunk(high), :], keyed[chunk(j), :], NT, preferred_element_type=f32)
             if t in (0, 8):
                 r = lax.broadcasted_iota(jnp.int32, s.shape, 0)
@@ -131,7 +135,7 @@
         g = group(steps[0])
         stat[g] = jnp.broadcast_to(jnp.max(stat[g], -1, keepdims=True), stat.shape[1:])
         for t in steps:
-            high, j = step_at(low, t)
+            high, j = step_at(low, doc, t)
             e = jnp.exp2((s_ref[:, cols(t)] - tiled(stat[g, chunk(high), :])) * C2)
             s_ref[:, cols(t)] = e
             delta[g, chunk(high), :] += lanes(e, jnp.add)
@@ -154,7 +158,7 @@
 
     def mix(steps):
         for t in steps:
-            high, j = step_at(low, t)
+            high, j = step_at(low, doc, t)
             w = (s_ref[:, cols(t)] * tiled(stat[group(t), chunk(high), :])).astype(bf16)
             w_ref[:, cols(t)] = w
             mixed[chunk(high), :] += jnp.dot(w, values(j), preferred_element_type=f32)
@@ -170,7 +174,7 @@
     return rs
 
 
-def backward(low, values, keyed, query, dmb, s_ref, w_ref, d_ref, stat, delta, dk, dv, dq, after):
+def backward(low, doc, values, keyed, query, dmb, s_ref, w_ref, d_ref, stat, delta, dk, dv, dq, after):
     def cols(t):
         return pl.ds(t * BLOCK, BLOCK)
 
@@ -181,7 +185,7 @@
 
     def dprobs(steps):
         for t in steps:
-            high, j = step_at(low, t)
+            high, j = step_at(low, doc, t)
             dp = lax.dot_general(dmb[chunk(high), :], values(j), NT, preferred_element_type=f32)
             d_ref[:, cols(t)] = dp
             delta[group(t), chunk(high), :] += lanes(dp * s_ref[:, cols(t)], jnp.add)
@@ -198,7 +202,7 @@
 
     def back(steps, far):
         for t in steps:
-            high, j = step_at(low, t)
+            high, j = step_at(low, doc, t)
             ds = ((s_ref[:, cols(t)] * tiled(stat[group(t), chunk(high), :]))
                   * (d_ref[:, cols(t)] - tiled(delta[0, chunk(high), :]))).astype(bf16)
             dvalue(t, high, j)
@@ -215,7 +219,7 @@
     back((5, 6), False)
     after(2)
     for t in (1, 2, 3, 4):
-        dquery(w_ref[:, cols(t)], *step_at(low, t))
+        dquery(w_ref[:, cols(t)], *step_at(low, doc, t))
     back((0, 8, 7), False)
     after(3)
 
@@ -239,6 +243,7 @@
     before = (seq + 127) % 128
     after = (seq + 1) % 128
     head = x * 8 + z
+    doc = y // 2
     by, bcore, _high = owner(before // 32, (before // 8) % 4, core)
     mine_before = (by == y) & (bcore == core)
     pending = []
@@ -411,7 +416,7 @@
         prepare(farsib)
         prepare(7 - farsib)
 
-    forward(low, values, keyed, query, s_ref, w_ref, stat, delta, mixed, early, sib_keys, far_keys, farsib_keys)
+    forward(low, doc, values, keyed, query, s_ref, w_ref, stat, delta, mixed, early, sib_keys, far_keys, farsib_keys)
     rs = normed(mixed, out_h)
 
     head_columns = pl.ds(pl.multiple_of(head * HEAD_DIM, HEAD_DIM), HEAD_DIM)
@@ -464,7 +469,7 @@
     outer = 1 - low // 2
 
     def in_turn(block, turn):
-        return block + ((turn + outer + 1) % 2) * (7 - 2 * block)
+        return block + ((turn + 1 + outer * (1 + doc)) % 2) * (7 - 2 * block)
 
     def combine(turn):
         to_sib[turn].wait_recv()
@@ -486,7 +491,7 @@
         if n in (1, 2):
             combine(n - 1)
 
-    backward(low, values, keyed, query, dmb, s_ref, w_ref, d_ref, stat, delta, dk, dv, dq, after_steps)
+    backward(low, doc, values, keyed, query, dmb, s_ref, w_ref, d_ref, stat, delta, dk, dv, dq, after_steps)
     gq = jnp.zeros((1, HEAD_DIM), f32)
     for i, block in enumerate((low, 7 - low)):
         gq = gq + jnp.sum(dq[chunk(i), :] * values(block).astype(f32), 0, keepdims=True)
@@ -503,7 +508,7 @@
     to_sib[2].wait_recv()
     to_sib[3].wait_recv()
     for turn in range(2):
-        high = (turn + outer) % 2
+        high = (turn + outer + (1 - outer) * doc) % 2
         mixed[chunk(high), :] = (dv[chunk(low + high * (7 - 2 * low)), :] + from_sib[2 + high]
                                  + dq[chunk(high), :] * qgain)
         to_partner[turn].wait_recv()

time: 61.5 us -> 61.5 us (level)
  no operation moved by 1% of the time
where the time goes in v6:
time: 61.5 us; the launch traced here: 61.3 us
  Pallas kernels  60.5 us (98%)
  between operations  0.8 us (1%)
    pallas_call x1, Pallas kernels, on_device(): pl.pallas_call(whole, out_shape=(shape(by_head, bf16), shape(by_head, bf1...  57.7 us
    pallas_call x1, Pallas kernels, on_device(): pl.pallas_call(finish, out_shape=(shape((128, width), f32), shape((PIECE,...  2.75 us

profile of v6, /device:TPU:1, one launch (start us, length us, event | category | flops | bytes accessed | tf_op | source)
XLA Modules:
  0.0 61.3 jit_solution(10388286416740138090)
XLA Ops:
  0.6 57.7 %shard_map.93 = (bf16[32,32,128]{2,1,0:T(8,128)(2,1)}, bf16[32,32,128]{2,1,0:T(8,128)(2,1)}, f32[1,4096]{1,0:T(1,128)}, f32[32,2,128]{2,1,0:T(2,128)}, f32[1,128]{1,0:T(1,128)}) custom-call(bf16[128,4096]{1,0:T(8,128)(2,1)} %bitcast.8, s32[1,32]{1,0:T(1,128)} %starts.3, s32[1,32]{1,0:T(1,128)} %lengths.3, f32[32,128]{1,0:T(8,128)} %bitcast.10, ...), custom_call_target="tpu_custom_call" | custom-call | tf_op jit(solution)/shard_map/pallas_call | solution.py:626
  58.4 2.8 %shard_map.94 = (f32[128,4096]{1,0:T(8,128)}, bf16[32,4096]{1,0:T(8,128)(2,1)}, f32[32,128]{1,0:T(8,128)}, f32[32,128]{1,0:T(8,128)}) custom-call(s32[1,32]{1,0:T(1,128)} %starts.3, s32[1,32]{1,0:T(1,128)} %lengths.3, bf16[32,32,128]{2,1,0:T(8,128)(2,1)} %get-tuple-element.13.dpool, f32[1,4096]{1,0:T(1,128)} %get-tuple-element.14.spill_back, ...), custom_call_target="tpu_custom_call" | custom-call | tf_op jit(solution)/shard_map/pallas_call | solution.py:652
